TPU v7x, 32 devices: a whole 2x2x4 slice. The times are simulated.
32 devices in a mesh: section: 2 (over x), seq: 4 (over y, core), dp: 4 (over z).
Axes of the slice: x: 2, y: 2, z: 4, core: 2. Of those that a mesh axis runs over, the one named last changes fastest.
Arguments:
- boundary: bfloat16 [2, 16, 1024, 1280], P('section', 'dp', 'seq'), may hold values from -6 to 6
- lengths: int32 [16, 4], P('dp'), may hold values from 0 to 1024, as said below
- masked: int32 [16, 1024], P('dp', 'seq'), may hold values 0 or 1
- residues: int32 [16, 1024], P('dp', 'seq'), may hold values from 0 to 29
- readout: bfloat16 [1280, 30], replicated, may hold values from -0.15625 to 0.15625
- first_gain: float32 [2, 1280], P('section'), may hold values from 0.5 to 1.5
- first_shift: float32 [2, 1280], P('section'), may hold values from -2 to 2
- in_weight: bfloat16 [2, 1280, 640], P('section'), may hold values from -0.15625 to 0.15625
- in_bias: float32 [2, 640], P('section'), may hold values from -2 to 2
- second_gain: float32 [2, 640], P('section'), may hold values from 0.5 to 1.5
- second_shift: float32 [2, 640], P('section'), may hold values from -2 to 2
- conv_weight: bfloat16 [2, 5, 640, 640], P('section'), may hold values from -0.109375 to 0.109375
- conv_bias: float32 [2, 640], P('section'), may hold values from -2 to 2
- third_gain: float32 [2, 640], P('section'), may hold values from 0.5 to 1.5
- third_shift: float32 [2, 640], P('section'), may hold values from -2 to 2
- out_weight: bfloat16 [2, 640, 1280], P('section'), may hold values from -0.25 to 0.25
- out_bias: float32 [2, 1280], P('section'), may hold values from -2 to 2
Outputs:
- boundary_out: bfloat16 [2, 16, 1024, 1280], P('section', 'dp', 'seq')
- grad_first_gain: float32 [2, 1280], P('section')
- grad_first_shift: float32 [2, 1280], P('section')
- grad_in_weight: float32 [2, 1280, 640], P('section')
- grad_in_bias: float32 [2, 640], P('section')
- grad_second_gain: float32 [2, 640], P('section')
- grad_second_shift: float32 [2, 640], P('section')
- grad_conv_weight: float32 [2, 5, 640, 640], P('section')
- grad_conv_bias: float32 [2, 640], P('section')
- grad_third_gain: float32 [2, 640], P('section')
- grad_third_shift: float32 [2, 640], P('section')
- grad_out_weight: float32 [2, 640, 1280], P('section')
- grad_out_bias: float32 [2, 1280], P('section')
- type_scores: float32 [30], replicated
- type_counts: int32 [30], replicated
Inputs may be any that keep to these rules, and one draw needn't show every extreme that they name: `lengths`: the items of a row lie one after another from position 0 and the rest of the row is padding; in each aligned block of 4 rows one row is a single item of 1024 positions.
All inputs are finite; a program needn't handle non-finite values. No bound on the sum of `masked` on one device may be relied on, other than what follows from the above.
Results may differ from a plain program's by a relative error of at most 0.012.
Values may be sent and summed in bfloat16 or wider, within the bound.
A program may use at most 256 MiB of HBM per device.

v0:
```python
import jax
import jax.numpy as jnp
from jax import lax
from jax.sharding import PartitionSpec as P

KERNEL = 5
VOCAB = 30
DILATION_STEP = 128
ITEMS = 4


EPSILON = 1e-05


def from_behind(value, axis, by):
    length = lax.axis_size(axis)
    pairs = [(i, i + by) for i in range(length) if 0 <= i + by < length]
    return lax.ppermute(value, axis, pairs)


def norm_act(values, gain, bias, genuine_rows):
    average = jnp.mean(values, axis=-1, keepdims=True)
    centred = values - average
    spread = jnp.mean(centred * centred, axis=-1, keepdims=True)
    normalized = centred * lax.rsqrt(spread + EPSILON) * gain + bias
    return jax.nn.gelu(normalized, approximate=False) * genuine_rows


def local_pullback(values, gain, bias, genuine_rows, cotangent):

    def piece(inner, inner_gain, inner_bias):
        return norm_act(inner, inner_gain, inner_bias, genuine_rows)

    result, pullback = jax.vjp(piece, values, gain, bias)
    return pullback(cotangent)


def conv_rims(values):
    pieces = []
    for offset in (2, 1, -1, -2):
        pieces.append(from_behind(values, "seq", offset))
    return jnp.concatenate([pieces[0], pieces[1], values, pieces[2], pieces[3]], axis=0)


def grad_rims(values):
    pieces = []
    for offset in (2, 1, -1, -2):
        pieces.append(from_behind(values, "seq", offset))
    return jnp.concatenate([pieces[0], pieces[1], values, pieces[2], pieces[3]], axis=0)


def make_context(lengths, batch_index, seq_first, positions, row_len):
    lengths_row = lengths[batch_index]
    item_ends = jnp.cumsum(lengths_row, dtype=jnp.int32)
    position_ids = seq_first - 2 * positions + jnp.arange(5 * positions, dtype=jnp.int32)
    segment_ext = jnp.sum(
        (position_ids[:, None] >= item_ends[None, :]).astype(jnp.int32), axis=1, dtype=jnp.int32
    )
    inside = (position_ids >= 0) & (position_ids < row_len)
    segment_ext = jnp.where(inside, segment_ext, -1)
    segment_own = segment_ext[2 * positions : 3 * positions]
    genuine_rows = ((segment_own >= 0) & (segment_own < ITEMS)).astype(jnp.float32)[:, None]
    return (segment_ext, segment_own, genuine_rows)


def tap_mask(segment_ext, segment_own, start, positions):
    other = lax.dynamic_slice_in_dim(segment_ext, start, positions, 0)
    valid = (other == segment_own) & (segment_own >= 0) & (segment_own < ITEMS)
    return valid.astype(jnp.bfloat16)[:, None]


def gather_taps(extended, segment_ext, segment_own, dilation_rate, positions, direction):
    taps = []
    for tap_index in range(KERNEL):
        start = 2 * positions + direction * (tap_index - 2) * dilation_rate
        piece = lax.dynamic_slice_in_dim(extended, start, positions, 0)
        taps.append(piece * tap_mask(segment_ext, segment_own, start, positions))
    return jnp.concatenate(taps, axis=1)


def forward_block(block_in, weights, context, dilation_rate):
    (
        first_gain,
        first_shift,
        in_weight,
        in_bias,
        second_gain,
        second_shift,
        conv_weight,
        conv_bias,
        third_gain,
        third_shift,
        out_weight,
        out_bias,
    ) = weights
    segment_ext, segment_own, genuine_rows = context
    positions = block_in.shape[0]
    values = block_in.astype(jnp.float32)
    first_act = norm_act(values, first_gain, first_shift, genuine_rows).astype(jnp.bfloat16)
    first_pre = jnp.dot(first_act, in_weight, preferred_element_type=jnp.float32) + in_bias
    second_act = norm_act(first_pre, second_gain, second_shift, genuine_rows).astype(jnp.bfloat16)
    extended = conv_rims(second_act)
    stacked = gather_taps(extended, segment_ext, segment_own, dilation_rate, positions, 1)
    conv_flat = conv_weight.reshape(-1, conv_weight.shape[2])
    second_pre = jnp.dot(stacked, conv_flat, preferred_element_type=jnp.float32) + conv_bias
    third_act = norm_act(second_pre, third_gain, third_shift, genuine_rows).astype(jnp.bfloat16)
    third_pre = jnp.dot(third_act, out_weight, preferred_element_type=jnp.float32) + out_bias
    block_out = (values + third_pre).astype(jnp.bfloat16)
    return (block_out, (values, first_act, first_pre, stacked, second_pre, third_act))


def backward_block(grad_out, kept, weights, context, dilation_rate):
    (
        first_gain,
        first_shift,
        in_weight,
        in_bias,
        second_gain,
        second_shift,
        conv_weight,
        conv_bias,
        third_gain,
        third_shift,
        out_weight,
        out_bias,
    ) = weights
    values, first_act, first_pre, stacked, second_pre, third_act = kept
    segment_ext, segment_own, genuine_rows = context
    positions = grad_out.shape[0]
    contract = (((0,), (0,)), ((), ()))
    grad_float = grad_out.astype(jnp.float32)
    grad_out_bias = jnp.sum(grad_float, axis=0)
    grad_out_weight = lax.dot_general(
        third_act, grad_out, contract, preferred_element_type=jnp.float32
    )
    grad_third_act = jnp.dot(grad_out, out_weight.T, preferred_element_type=jnp.float32)
    grad_second_pre, grad_third_gain, grad_third_shift = local_pullback(
        second_pre, third_gain, third_shift, genuine_rows, grad_third_act
    )
    grad_second_low = grad_second_pre.astype(jnp.bfloat16)
    grad_conv_bias = jnp.sum(grad_second_low, axis=0, dtype=jnp.float32)
    grad_conv_weight = lax.dot_general(
        stacked, grad_second_low, contract, preferred_element_type=jnp.float32
    ).reshape(conv_weight.shape)
    grad_extended = grad_rims(grad_second_low)
    back_stacked = gather_taps(
        grad_extended, segment_ext, segment_own, dilation_rate, positions, -1
    )
    conv_back = jnp.transpose(conv_weight, (0, 2, 1)).reshape(-1, conv_weight.shape[1])
    grad_second_act = jnp.dot(back_stacked, conv_back, preferred_element_type=jnp.float32)
    grad_first_pre, grad_second_gain, grad_second_shift = local_pullback(
        first_pre, second_gain, second_shift, genuine_rows, grad_second_act
    )
    grad_first_low = grad_first_pre.astype(jnp.bfloat16)
    grad_in_bias = jnp.sum(grad_first_low, axis=0, dtype=jnp.float32)
    grad_in_weight = lax.dot_general(
        first_act, grad_first_low, contract, preferred_element_type=jnp.float32
    )
    grad_first_act = jnp.dot(grad_first_low, in_weight.T, preferred_element_type=jnp.float32)
    grad_values, grad_first_gain, grad_first_shift = local_pullback(
        values, first_gain, first_shift, genuine_rows, grad_first_act
    )
    grad_in = (grad_float + grad_values).astype(jnp.bfloat16)
    return (
        grad_in,
        (
            grad_first_gain,
            grad_first_shift,
            grad_in_weight,
            grad_in_bias,
            grad_second_gain,
            grad_second_shift,
            grad_conv_weight,
            grad_conv_bias,
            grad_third_gain,
            grad_third_shift,
            grad_out_weight,
            grad_out_bias,
        ),
    )


def shards(
    boundary,
    lengths,
    masked,
    residues,
    readout,
    first_gain,
    first_shift,
    in_weight,
    in_bias,
    second_gain,
    second_shift,
    conv_weight,
    conv_bias,
    third_gain,
    third_shift,
    out_weight,
    out_bias,
):
    weights = tuple(
        (
            item[0]
            for item in (
                first_gain,
                first_shift,
                in_weight,
                in_bias,
                second_gain,
                second_shift,
                conv_weight,
                conv_bias,
                third_gain,
                third_shift,
                out_weight,
                out_bias,
            )
        )
    )
    section_index = lax.axis_index("section")
    leading_section = section_index == 0
    last_section = section_index == lax.axis_size("section") - 1
    micro_count = boundary.shape[1]
    positions = boundary.shape[2]
    width = boundary.shape[3]
    row_len = positions * lax.axis_size("seq")
    seq_first = lax.axis_index("seq") * positions
    dilation_rate = jnp.where(leading_section, 1, DILATION_STEP)
    vocab_ids = jnp.arange(VOCAB, dtype=jnp.int32)
    incoming = jnp.zeros((positions, width), jnp.bfloat16)
    seen_inputs = []
    kept_list = []
    outputs = []
    type_hits = jnp.zeros((VOCAB,), jnp.float32)
    type_tally = jnp.zeros((VOCAB,), jnp.float32)
    for time_step in range(micro_count + 1):
        offset_index = time_step - section_index
        active = (offset_index >= 0) & (offset_index < micro_count)
        batch_index = jnp.clip(offset_index, 0, micro_count - 1)
        block_in = jnp.where(
            leading_section, boundary[0, min(time_step, micro_count - 1)], incoming
        )
        context = make_context(lengths, batch_index, seq_first, positions, row_len)
        block_out, kept = forward_block(block_in, weights, context, dilation_rate)
        seen_inputs.append(block_in)
        kept_list.append(kept)
        outputs.append(block_out)
        logits = jnp.dot(block_out, readout, preferred_element_type=jnp.float32)
        probability = jax.nn.softmax(logits, axis=-1)
        one_hot = (residues[batch_index][:, None] == vocab_ids[None, :]).astype(jnp.float32)
        chosen = (
            masked[batch_index].astype(jnp.float32)
            * context[2][:, 0]
            * (active & last_section).astype(jnp.float32)
        )
        truth = jnp.sum(one_hot * probability, axis=1)
        type_hits = type_hits + jnp.sum(one_hot * (chosen * truth)[:, None], axis=0)
        type_tally = type_tally + jnp.sum(one_hot * chosen[:, None], axis=0)
        if time_step < micro_count:
            incoming = from_behind(block_out, "section", 1)
    grad_totals = tuple((jnp.zeros(item.shape, jnp.float32) for item in weights))
    incoming_grad = jnp.zeros((positions, width), jnp.bfloat16)
    input_grads = []
    for time_step in range(micro_count + 1):
        offset_index = time_step - 1 + section_index
        active = (offset_index >= 0) & (offset_index < micro_count)
        batch_index = jnp.clip(offset_index, 0, micro_count - 1)
        lower_step = min(max(time_step - 1, 0), micro_count)
        upper_step = min(time_step + 1, micro_count)
        context = make_context(lengths, batch_index, seq_first, positions, row_len)
        kept = jax.tree.map(
            lambda early, later: jnp.where(leading_section, early, later),
            kept_list[lower_step],
            kept_list[upper_step],
        )
        grad_out = jnp.where(
            leading_section, incoming_grad, boundary[0, min(time_step, micro_count - 1)]
        )
        grad_in, grads = backward_block(grad_out, kept, weights, context, dilation_rate)
        grad_totals = tuple(
            (total + jnp.where(active, grad, 0.0) for total, grad in zip(grad_totals, grads))
        )
        input_grads.append(grad_in)
        if time_step < micro_count:
            incoming_grad = from_behind(grad_in, "section", -1)
    ends_grad = jnp.stack(input_grads[1:], axis=0)
    ends_out = jnp.stack(outputs[1:], axis=0)
    boundary_out = jnp.where(leading_section, ends_grad, ends_out)[None]
    flattened = tuple((total.reshape(1, -1) for total in grad_totals))
    summed = lax.psum(flattened, ("seq", "dp"))
    (
        grad_first_gain,
        grad_first_shift,
        grad_in_weight,
        grad_in_bias,
        grad_second_gain,
        grad_second_shift,
        grad_conv_weight,
        grad_conv_bias,
        grad_third_gain,
        grad_third_shift,
        grad_out_weight,
        grad_out_bias,
    ) = tuple((total.reshape((1,) + item.shape) for total, item in zip(summed, weights)))
    type_hits, type_tally = lax.psum((type_hits, type_tally), ("section", "seq", "dp"))
    type_scores = type_hits / jnp.maximum(type_tally, 1.0)
    type_counts = type_tally.astype(jnp.int32)
    return (
        boundary_out,
        grad_first_gain,
        grad_first_shift,
        grad_in_weight,
        grad_in_bias,
        grad_second_gain,
        grad_second_shift,
        grad_conv_weight,
        grad_conv_bias,
        grad_third_gain,
        grad_third_shift,
        grad_out_weight,
        grad_out_bias,
        type_scores,
        type_counts,
    )


def solution(mesh):
    in_specs = (
        P("section", "dp", "seq", None),
        P("dp", None),
        P("dp", "seq"),
        P("dp", "seq"),
        P(),
        P("section", None),
        P("section", None),
        P("section", None, None),
        P("section", None),
        P("section", None),
        P("section", None),
        P("section", None, None, None),
        P("section", None),
        P("section", None),
        P("section", None),
        P("section", None, None),
        P("section", None),
    )
    out_specs = (
        P("section", "dp", "seq", None),
        P("section", None),
        P("section", None),
        P("section", None, None),
        P("section", None),
        P("section", None),
        P("section", None),
        P("section", None, None, None),
        P("section", None),
        P("section", None),
        P("section", None),
        P("section", None, None),
        P("section", None),
        P(),
        P(),
    )
    return jax.shard_map(shards, mesh=mesh, in_specs=in_specs, out_specs=out_specs, check_vma=False)
```

profile of v0, /device:TPU:0, one launch (start us, length us, event | category | flops | bytes accessed | tf_op | source)
XLA Modules:
  0.0 755.0 jit_solution(12653033019115867903)
XLA Ops:
  12.5 5.0 fusion.719
  22.1 3.7 collective-permute-start.1
  25.9 5.1 collective-permute-start
  36.2 7.8 %copy.33 = bf16[1,5,640,640]{2,3,1,0:T(8,128)(2,1)} copy(bf16[1,5,640,640]{3,2,1,0:T(8,128)(2,1)} %param.28) | data formatting | bytes 8192000 | tf_op args[11]
  55.2 5.0 collective-permute-start.4
  61.3 11.6 %collective-permute-done.4 = bf16[256,1280]{1,0:T(8,128)(2,1)S(1)} collective-permute-done((bf16[256,1280]{1,0:T(8,128)(2,1)S(1)}, bf16[256,1280]{1,0:T(8,128)(2,1)S(1)}, u32[]{:S(2)}, u32[]{:S(2)}) %collective-permute-start.4) | collective-permute-done | bytes 655392 | tf_op jit(solution)/shard_map/ppermute | solution.py:18
  73.6 3.5 fusion.109
  82.4 3.1 collective-permute-start.6
  85.4 4.6 collective-permute-start.5
  90.2 7.9 %collective-permute-done.5 = bf16[256,640]{1,0:T(8,128)(2,1)S(1)} collective-permute-done((bf16[256,640]{1,0:T(8,128)(2,1)S(1)}, bf16[256,640]{1,0:T(8,128)(2,1)S(1)}, u32[]{:S(2)}, u32[]{:S(2)}) %collective-permute-start.5) | collective-permute-done | bytes 327712 | tf_op jit(solution)/shard_map/ppermute | solution.py:18
  103.9 4.4 collective-permute-start.14
  108.6 2.9 multiply_reduce_fusion.19
  115.1 3.1 collective-permute-start.10
  118.2 4.8 collective-permute-start.9
  123.0 4.7 fusion.58
  133.2 3.6 multiply_reduce_fusion.24
  139.5 5.0 multiply_reduce_fusion.4
  144.9 3.7 fusion.100
  153.9 3.1 collective-permute-start.16
  157.0 4.5 collective-permute-start.15
  161.8 7.9 %collective-permute-done.15 = bf16[256,640]{1,0:T(8,128)(2,1)S(1)} collective-permute-done((bf16[256,640]{1,0:T(8,128)(2,1)S(1)}, bf16[256,640]{1,0:T(8,128)(2,1)S(1)}, u32[]{:S(2)}, u32[]{:S(2)}) %collective-permute-start.15) | collective-permute-done | bytes 327712 | tf_op jit(solution)/shard_map/ppermute | solution.py:18
  177.8 14.0 %collective-permute-done.24 = bf16[256,1280]{1,0:T(8,128)(2,1)S(1)} collective-permute-done((bf16[256,1280]{1,0:T(8,128)(2,1)S(1)}, bf16[256,1280]{1,0:T(8,128)(2,1)S(1)}, u32[]{:S(2)}, u32[]{:S(2)}) %collective-permute-start.24) | collective-permute-done | bytes 655392 | tf_op jit(solution)/shard_map/ppermute | solution.py:18
  191.7 5.1 fusion.294
  197.7 3.5 fusion.91
  206.5 3.1 collective-permute-start.26
  209.5 4.6 collective-permute-start.25
  216.1 6.2 collective-permute-done.25
  225.3 6.8 collective-permute-done.13
  233.0 2.9 multiply_reduce_fusion.18
  241.2 3.1 collective-permute-start.20
  244.2 4.6 collective-permute-start.19
  251.6 4.7 fusion.56
  258.2 3.7 multiply_reduce_fusion.23
  262.4 3.8 fusion.144
  271.2 16.0 %collective-permute-done.23 = bf16[256,1280]{1,0:T(8,128)(2,1)S(1)} collective-permute-done((bf16[256,1280]{1,0:T(8,128)(2,1)S(1)}, bf16[256,1280]{1,0:T(8,128)(2,1)S(1)}, u32[]{:S(2)}, u32[]{:S(2)}) %collective-permute-start.23) | collective-permute-done | bytes 655392 | tf_op jit(solution)/shard_map/ppermute | solution.py:18
  287.4 2.9 multiply_reduce_fusion.17
  293.9 3.1 collective-permute-start.30
  296.9 4.6 collective-permute-start.29
  301.5 4.7 fusion.54
  310.7 3.6 multiply_reduce_fusion.22
  315.4 5.2 multiply_reduce_fusion.2
  320.9 4.1 fusion.695
  330.4 3.1 collective-permute-start.36
  333.5 4.5 collective-permute-start.35
  351.4 5.6 collective-permute-done.33
  357.3 2.9 multiply_reduce_fusion.16
  367.3 3.6 collective-permute-done.39
  371.1 4.8 collective-permute-done.42
  376.7 3.7 multiply_reduce_fusion.21
  381.4 5.0 multiply_reduce_fusion.1
  391.0 4.9 fusion.52
  395.8 8.3 %collective-permute-done.43 = bf16[256,1280]{1,0:T(8,128)(2,1)S(1)} collective-permute-done((bf16[256,1280]{1,0:T(8,128)(2,1)S(1)}, bf16[256,1280]{1,0:T(8,128)(2,1)S(1)}, u32[]{:S(2)}, u32[]{:S(2)}) %collective-permute-start.43) | collective-permute-done | bytes 655392 | tf_op jit(solution)/shard_map/ppermute | solution.py:18
  405.0 2.9 multiply_reduce_fusion.15
  412.2 5.7 collective-permute-start.45
  417.9 5.2 collective-permute-start.44
  425.5 15.3 %select_add_fusion = f32[3200,640]{1,0:T(8,128)} fusion(f32[3200,640]{1,0:T(8,128)} %fusion.52, f32[3200,640]{1,0:T(8,128)} %fusion.54, f32[3200,640]{1,0:T(8,128)} %fusion.56, f32[3200,640]{1,0:T(8,128)S(1)} %bitcast.344, bf16[256,640]{1,0:T(8,128)(2,1)} %get-tuple-element.133, pred[]{:T(512)S(6)} %and.444, pred[]{:T(512)S(6)} %and.443, pred[]{:T(512)S(6)} %and.442, ...), kind=kOutput, calls=%fused_computation | convolution fusion | flops 1067827200 | bytes 44564488 | tf_op jit(solution)/shard_map/dot_general | solution.py:142
  440.8 7.7 %fusion.8 = f32[1,640,1280]{2,1,0:T(8,128)} fusion(f32[640,1280]{1,0:T(8,128)} %convolution_select_fusion, f32[640,1280]{1,0:T(8,128)} %convolution_select_fusion.1, f32[640,1280]{1,0:T(8,128)} %convolution_select_fusion.2, f32[640,1280]{1,0:T(8,128)} %convolution_select_fusion.4, bf16[256,1280]{1,0:T(8,128)(2,1)} %copy-done.9, pred[]{:T(512)S(6)} %and.441, ...), kind=kOutput, calls=%fused_computation.19 | convolution fusion | flops 423690240 | bytes 17694722 | tf_op jit(solution)/shard_map/dot_general | solution.py:133
  455.9 3.2 multiply_reduce_fusion.20
  471.6 41.4 %all-reduce = (f32[30]{0:T(128)S(1)}, f32[30]{0:T(128)S(1)}) all-reduce(f32[30]{0:T(128)S(1)} %add_add_fusion.16, f32[30]{0:T(128)S(1)} %add_add_fusion.15), channel_id=1, replica_groups=mesh['section'=2,'seq'=4,'dp'=4] {'section','seq','dp'}, use_global_device_ids=true, to_apply=%region_187.188 | all-reduce | flops 60 | bytes 480 | tf_op jit(solution)/shard_map/psum | solution.py:306
  514.1 6.1 multiply_reduce_fusion
  520.3 64.5 %all-reduce.1 = (f32[1,1280]{1,0:T(1,128)}, f32[1,1280]{1,0:T(1,128)}, f32[1,640]{1,0:T(1,128)}, f32[1,640]{1,0:T(1,128)}, f32[1,640]{1,0:T(1,128)}, /*index=5*/...) all-reduce(f32[1,1280]{1,0:T(1,128)S(1)} %reshape.1819, ...), channel_id=1, replica_groups=mesh['section'=2,'seq'=4,'dp'=4] {'seq','dp'}, use_global_device_ids=true, to_apply=%region_115.116 | all-reduce | flops 7680 | bytes 61440 | tf_op jit(solution)/shard_map/psum | solution.py:291
  590.4 144.7 %all-reduce.5.cloned.1.call-done = (f32[1,1280,640]{2,1,0:T(8,128)}, f32[1,5,640,640]{3,2,1,0:T(8,128)}, f32[1,640,1280]{2,1,0:T(8,128)}) async-done(((f32[1,1280,640]{2,1,0:T(8,128)}, f32[1,5,640,640]{3,2,1,0:T(8,128)}, f32[1,640,1280]{2,1,0:T(8,128)}), (f32[1,1280,640]{2,1,0:T(8,128)}, f32[1,5,640,640]{3,2,1,0:T(8,128)}, f32[1,640,1280]{2,1,0:T(8,128)})) %all-reduce.5.cloned.1.call-update) | async-done | bytes 14745616 | tf_op jit(solution)/shard_map/psum | solution.py:291
  735.0 3.8 copy.117
  738.9 7.3 copy.118
  (738 shorter events, 167.8 us)
Async XLA Ops:
  7.3 727.8 %all-reduce.5.cloned.1.call-start = ((), (), s32[]{:S(2)}) async-start(), calls=%async_computation | async-start | bytes 29491200 | tf_op jit(solution)/shard_map/psum | solution.py:291
  19.5 29.0 %collective-permute-start.3 = (bf16[256,640]{1,0:T(8,128)(2,1)S(1)}, bf16[256,640]{1,0:T(8,128)(2,1)S(1)}, u32[]{:S(2)}, u32[]{:S(2)}) collective-permute-start(bf16[256,640]{1,0:T(8,128)(2,1)S(1)} %fusion.302), channel_id=1, source_target_pairs={{8,0},{12,4},{9,1},{13,5},{10,2},{14,6},{11,3},{15,7},{24,16},{28,... | collective-permute-start | bytes 983048 | tf_op jit(solution)/shard_map/ppermute | solution.py:18
  20.8 27.7 %collective-permute-start.2 = (bf16[256,640]{1,0:T(8,128)(2,1)S(1)}, bf16[256,640]{1,0:T(8,128)(2,1)S(1)}, u32[]{:S(2)}, u32[]{:S(2)}) collective-permute-start(bf16[256,640]{1,0:T(8,128)(2,1)S(1)} %fusion.302), channel_id=1, source_target_pairs={{4,0},{8,4},{12,8},{5,1},{9,5},{13,9},{6,2},{10,6},{14,10},{7,3},{... | collective-permute-start | bytes 983048 | tf_op jit(solution)/shard_map/ppermute | solution.py:18
  22.1 23.6 %collective-permute-start.1 = (bf16[256,640]{1,0:T(8,128)(2,1)S(1)}, bf16[256,640]{1,0:T(8,128)(2,1)}, u32[]{:S(2)}, u32[]{:S(2)}) collective-permute-start(bf16[256,640]{1,0:T(8,128)(2,1)S(1)} %fusion.302), channel_id=1, source_target_pairs={{0,4},{4,8},{8,12},{1,5},{5,9},{9,13},{2,6},{6,10},{10,14},{3,7},{... | collective-permute-start | bytes 983048 | tf_op jit(solution)/shard_map/ppermute | solution.py:18
  25.9 18.9 %collective-permute-start = (bf16[256,640]{1,0:T(8,128)(2,1)S(1)}, bf16[256,640]{1,0:T(8,128)(2,1)}, u32[]{:S(2)}, u32[]{:S(2)}) collective-permute-start(bf16[256,640]{1,0:T(8,128)(2,1)S(1)} %fusion.302), channel_id=1, source_target_pairs={{0,8},{4,12},{1,9},{5,13},{2,10},{6,14},{3,11},{7,15},{16,24},{20,... | collective-permute-start | bytes 983048 | tf_op jit(solution)/shard_map/ppermute | solution.py:18
  31.2 217.7 %copy-start.70 = (f32[1280]{0:T(1024)}, f32[1280]{0:T(1024)S(1)}, u32[]{:S(2)}) copy-start(f32[1280]{0:T(1024)S(1)} %reduce.9) | copy-start | bytes 15364
  54.5 73.2 %copy-start.27 = (bf16[256,640]{1,0:T(8,128)(2,1)}, bf16[256,640]{1,0:T(8,128)(2,1)S(1)}, u32[]{:S(2)}) copy-start(bf16[256,640]{1,0:T(8,128)(2,1)S(1)} %fusion.306) | copy-start | bytes 983044
  55.2 17.8 %collective-permute-start.4 = (bf16[256,1280]{1,0:T(8,128)(2,1)S(1)}, bf16[256,1280]{1,0:T(8,128)(2,1)S(1)}, u32[]{:S(2)}, u32[]{:S(2)}) collective-permute-start(bf16[256,1280]{1,0:T(8,128)(2,1)S(1)} %fusion.19), channel_id=1, source_target_pairs={{0,16},{1,17},{2,18},{3,19},{4,20},{5,21},{6,22},{7,23},{8,24},{9,... | collective-permute-start | bytes 1966088 | tf_op jit(solution)/shard_map/ppermute | solution.py:18
  79.8 18.6 %collective-permute-start.8 = (bf16[256,640]{1,0:T(8,128)(2,1)S(1)}, bf16[256,640]{1,0:T(8,128)(2,1)S(1)}, u32[]{:S(2)}, u32[]{:S(2)}) collective-permute-start(bf16[256,640]{1,0:T(8,128)(2,1)S(1)} %get-tuple-element.223), channel_id=1, source_target_pairs={{8,0},{12,4},{9,1},{13,5},{10,2},{14,6},{11,3},{15,7},{24,16},{28,... | collective-permute-start | bytes 983048 | tf_op jit(solution)/shard_map/ppermute | solution.py:18
  81.1 17.2 %collective-permute-start.7 = (bf16[256,640]{1,0:T(8,128)(2,1)S(1)}, bf16[256,640]{1,0:T(8,128)(2,1)S(1)}, u32[]{:S(2)}, u32[]{:S(2)}) collective-permute-start(bf16[256,640]{1,0:T(8,128)(2,1)S(1)} %get-tuple-element.223), channel_id=1, source_target_pairs={{4,0},{8,4},{12,8},{5,1},{9,5},{13,9},{6,2},{10,6},{14,10},{7,3},{... | collective-permute-start | bytes 983048 | tf_op jit(solution)/shard_map/ppermute | solution.py:18
  82.4 15.8 %collective-permute-start.6 = (bf16[256,640]{1,0:T(8,128)(2,1)S(1)}, bf16[256,640]{1,0:T(8,128)(2,1)S(1)}, u32[]{:S(2)}, u32[]{:S(2)}) collective-permute-start(bf16[256,640]{1,0:T(8,128)(2,1)S(1)} %get-tuple-element.223), channel_id=1, source_target_pairs={{0,4},{4,8},{8,12},{1,5},{5,9},{9,13},{2,6},{6,10},{10,14},{3,7},{... | collective-permute-start | bytes 983048 | tf_op jit(solution)/shard_map/ppermute | solution.py:18
  85.4 12.7 %collective-permute-start.5 = (bf16[256,640]{1,0:T(8,128)(2,1)S(1)}, bf16[256,640]{1,0:T(8,128)(2,1)S(1)}, u32[]{:S(2)}, u32[]{:S(2)}) collective-permute-start(bf16[256,640]{1,0:T(8,128)(2,1)S(1)} %get-tuple-element.223), channel_id=1, source_target_pairs={{0,8},{4,12},{1,9},{5,13},{2,10},{6,14},{3,11},{7,15},{16,24},{20,... | collective-permute-start | bytes 983048 | tf_op jit(solution)/shard_map/ppermute | solution.py:18
  103.9 34.0 %collective-permute-start.14 = (bf16[256,1280]{1,0:T(8,128)(2,1)S(1)}, bf16[256,1280]{1,0:T(8,128)(2,1)S(1)}, u32[]{:S(2)}, u32[]{:S(2)}) collective-permute-start(bf16[256,1280]{1,0:T(8,128)(2,1)S(1)} %fusion.15), channel_id=1, source_target_pairs={{0,16},{1,17},{2,18},{3,19},{4,20},{5,21},{6,22},{7,23},{8,24},{9,... | collective-permute-start | bytes 1966088 | tf_op jit(solution)/shard_map/ppermute | solution.py:18
  112.5 18.6 %collective-permute-start.12 = (bf16[256,640]{1,0:T(8,128)(2,1)S(1)}, bf16[256,640]{1,0:T(8,128)(2,1)S(1)}, u32[]{:S(2)}, u32[]{:S(2)}) collective-permute-start(bf16[256,640]{1,0:T(8,128)(2,1)S(1)} %get-tuple-element.125), channel_id=1, source_target_pairs={{8,0},{12,4},{9,1},{13,5},{10,2},{14,6},{11,3},{15,7},{24,16},{28,... | collective-permute-start | bytes 983048 | tf_op jit(solution)/shard_map/ppermute | solution.py:18
  113.8 17.3 %collective-permute-start.11 = (bf16[256,640]{1,0:T(8,128)(2,1)S(1)}, bf16[256,640]{1,0:T(8,128)(2,1)S(1)}, u32[]{:S(2)}, u32[]{:S(2)}) collective-permute-start(bf16[256,640]{1,0:T(8,128)(2,1)S(1)} %get-tuple-element.125), channel_id=1, source_target_pairs={{4,0},{8,4},{12,8},{5,1},{9,5},{13,9},{6,2},{10,6},{14,10},{7,3},{... | collective-permute-start | bytes 983048 | tf_op jit(solution)/shard_map/ppermute | solution.py:18
  115.1 15.8 %collective-permute-start.10 = (bf16[256,640]{1,0:T(8,128)(2,1)S(1)}, bf16[256,640]{1,0:T(8,128)(2,1)S(1)}, u32[]{:S(2)}, u32[]{:S(2)}) collective-permute-start(bf16[256,640]{1,0:T(8,128)(2,1)S(1)} %get-tuple-element.125), channel_id=1, source_target_pairs={{0,4},{4,8},{8,12},{1,5},{5,9},{9,13},{2,6},{6,10},{10,14},{3,7},{... | collective-permute-start | bytes 983048 | tf_op jit(solution)/shard_map/ppermute | solution.py:18
  118.2 12.7 %collective-permute-start.9 = (bf16[256,640]{1,0:T(8,128)(2,1)S(1)}, bf16[256,640]{1,0:T(8,128)(2,1)S(1)}, u32[]{:S(2)}, u32[]{:S(2)}) collective-permute-start(bf16[256,640]{1,0:T(8,128)(2,1)S(1)} %get-tuple-element.125), channel_id=1, source_target_pairs={{0,8},{4,12},{1,9},{5,13},{2,10},{6,14},{3,11},{7,15},{16,24},{20,... | collective-permute-start | bytes 983048 | tf_op jit(solution)/shard_map/ppermute | solution.py:18
  148.6 121.8 %copy-start.12 = (bf16[256,1280]{1,0:T(8,128)(2,1)}, bf16[256,1280]{1,0:T(8,128)(2,1)S(1)}, u32[]{:S(2)}) copy-start(bf16[256,1280]{1,0:T(8,128)(2,1)S(1)} %fusion.100) | copy-start | bytes 1966084
  151.3 18.6 %collective-permute-start.18 = (bf16[256,640]{1,0:T(8,128)(2,1)S(1)}, bf16[256,640]{1,0:T(8,128)(2,1)S(1)}, u32[]{:S(2)}, u32[]{:S(2)}) collective-permute-start(bf16[256,640]{1,0:T(8,128)(2,1)S(1)} %get-tuple-element.221), channel_id=1, source_target_pairs={{8,0},{12,4},{9,1},{13,5},{10,2},{14,6},{11,3},{15,7},{24,16},{28,... | collective-permute-start | bytes 983048 | tf_op jit(solution)/shard_map/ppermute | solution.py:18
  152.6 17.2 %collective-permute-start.17 = (bf16[256,640]{1,0:T(8,128)(2,1)S(1)}, bf16[256,640]{1,0:T(8,128)(2,1)S(1)}, u32[]{:S(2)}, u32[]{:S(2)}) collective-permute-start(bf16[256,640]{1,0:T(8,128)(2,1)S(1)} %get-tuple-element.221), channel_id=1, source_target_pairs={{4,0},{8,4},{12,8},{5,1},{9,5},{13,9},{6,2},{10,6},{14,10},{7,3},{... | collective-permute-start | bytes 983048 | tf_op jit(solution)/shard_map/ppermute | solution.py:18
  153.9 15.8 %collective-permute-start.16 = (bf16[256,640]{1,0:T(8,128)(2,1)S(1)}, bf16[256,640]{1,0:T(8,128)(2,1)S(1)}, u32[]{:S(2)}, u32[]{:S(2)}) collective-permute-start(bf16[256,640]{1,0:T(8,128)(2,1)S(1)} %get-tuple-element.221), channel_id=1, source_target_pairs={{0,4},{4,8},{8,12},{1,5},{5,9},{9,13},{2,6},{6,10},{10,14},{3,7},{... | collective-permute-start | bytes 983048 | tf_op jit(solution)/shard_map/ppermute | solution.py:18
  157.0 12.7 %collective-permute-start.15 = (bf16[256,640]{1,0:T(8,128)(2,1)S(1)}, bf16[256,640]{1,0:T(8,128)(2,1)S(1)}, u32[]{:S(2)}, u32[]{:S(2)}) collective-permute-start(bf16[256,640]{1,0:T(8,128)(2,1)S(1)} %get-tuple-element.221), channel_id=1, source_target_pairs={{0,8},{4,12},{1,9},{5,13},{2,10},{6,14},{3,11},{7,15},{16,24},{20,... | collective-permute-start | bytes 983048 | tf_op jit(solution)/shard_map/ppermute | solution.py:18
  174.4 214.2 %copy-start.26 = (bf16[256,640]{1,0:T(8,128)(2,1)}, bf16[256,640]{1,0:T(8,128)(2,1)S(1)}, u32[]{:S(2)}) copy-start(bf16[256,640]{1,0:T(8,128)(2,1)S(1)} %get-tuple-element.220) | copy-start | bytes 983044
  175.4 16.3 %collective-permute-start.24 = (bf16[256,1280]{1,0:T(8,128)(2,1)S(1)}, bf16[256,1280]{1,0:T(8,128)(2,1)S(1)}, u32[]{:S(2)}, u32[]{:S(2)}) collective-permute-start(bf16[256,1280]{1,0:T(8,128)(2,1)S(1)} %fusion.16), channel_id=1, source_target_pairs={{0,16},{1,17},{2,18},{3,19},{4,20},{5,21},{6,22},{7,23},{8,24},{9,... | collective-permute-start | bytes 1966088 | tf_op jit(solution)/shard_map/ppermute | solution.py:18
  196.8 184.6 %copy-start.2 = (bf16[256,1280]{1,0:T(8,128)(2,1)}, bf16[256,1280]{1,0:T(8,128)(2,1)S(1)}, u32[]{:S(2)}) copy-start(bf16[256,1280]{1,0:T(8,128)(2,1)S(1)} %get-tuple-element.182) | copy-start | bytes 1966084
  201.2 136.9 %copy-start.18 = (bf16[256,1280]{1,0:T(8,128)(2,1)}, bf16[256,1280]{1,0:T(8,128)(2,1)S(1)}, u32[]{:S(2)}) copy-start(bf16[256,1280]{1,0:T(8,128)(2,1)S(1)} %fusion.91) | copy-start | bytes 1966084
  203.9 18.6 %collective-permute-start.28 = (bf16[256,640]{1,0:T(8,128)(2,1)S(1)}, bf16[256,640]{1,0:T(8,128)(2,1)S(1)}, u32[]{:S(2)}, u32[]{:S(2)}) collective-permute-start(bf16[256,640]{1,0:T(8,128)(2,1)S(1)} %get-tuple-element.218), channel_id=1, source_target_pairs={{8,0},{12,4},{9,1},{13,5},{10,2},{14,6},{11,3},{15,7},{24,16},{28,... | collective-permute-start | bytes 983048 | tf_op jit(solution)/shard_map/ppermute | solution.py:18
  205.2 17.2 %collective-permute-start.27 = (bf16[256,640]{1,0:T(8,128)(2,1)S(1)}, bf16[256,640]{1,0:T(8,128)(2,1)S(1)}, u32[]{:S(2)}, u32[]{:S(2)}) collective-permute-start(bf16[256,640]{1,0:T(8,128)(2,1)S(1)} %get-tuple-element.218), channel_id=1, source_target_pairs={{4,0},{8,4},{12,8},{5,1},{9,5},{13,9},{6,2},{10,6},{14,10},{7,3},{... | collective-permute-start | bytes 983048 | tf_op jit(solution)/shard_map/ppermute | solution.py:18
  206.5 15.8 %collective-permute-start.26 = (bf16[256,640]{1,0:T(8,128)(2,1)S(1)}, bf16[256,640]{1,0:T(8,128)(2,1)S(1)}, u32[]{:S(2)}, u32[]{:S(2)}) collective-permute-start(bf16[256,640]{1,0:T(8,128)(2,1)S(1)} %get-tuple-element.218), channel_id=1, source_target_pairs={{0,4},{4,8},{8,12},{1,5},{5,9},{9,13},{2,6},{6,10},{10,14},{3,7},{... | collective-permute-start | bytes 983048 | tf_op jit(solution)/shard_map/ppermute | solution.py:18
  209.5 12.7 %collective-permute-start.25 = (bf16[256,640]{1,0:T(8,128)(2,1)S(1)}, bf16[256,640]{1,0:T(8,128)(2,1)S(1)}, u32[]{:S(2)}, u32[]{:S(2)}) collective-permute-start(bf16[256,640]{1,0:T(8,128)(2,1)S(1)} %get-tuple-element.218), channel_id=1, source_target_pairs={{0,8},{4,12},{1,9},{5,13},{2,10},{6,14},{3,11},{7,15},{16,24},{20,... | collective-permute-start | bytes 983048 | tf_op jit(solution)/shard_map/ppermute | solution.py:18
  214.4 17.8 %collective-permute-start.13 = (bf16[256,1280]{1,0:T(8,128)(2,1)S(1)}, bf16[256,1280]{1,0:T(8,128)(2,1)S(1)}, u32[]{:S(2)}, u32[]{:S(2)}) collective-permute-start(bf16[256,1280]{1,0:T(8,128)(2,1)S(1)} %fusion.120), channel_id=1, source_target_pairs={{16,0},{17,1},{18,2},{19,3},{20,4},{21,5},{22,6},{23,7},{24,8},{25... | collective-permute-start | bytes 1966088 | tf_op jit(solution)/shard_map/ppermute | solution.py:18
  223.5 78.0 %copy-start.7 = (bf16[256,3200]{1,0:T(8,128)(2,1)}, bf16[256,3200]{1,0:T(8,128)(2,1)S(1)}, u32[]{:S(2)}) copy-start(bf16[256,3200]{1,0:T(8,128)(2,1)S(1)} %multiply_dynamic-update-slice_fusion.20) | copy-start | bytes 4915204
  238.6 18.6 %collective-permute-start.22 = (bf16[256,640]{1,0:T(8,128)(2,1)S(1)}, bf16[256,640]{1,0:T(8,128)(2,1)S(1)}, u32[]{:S(2)}, u32[]{:S(2)}) collective-permute-start(bf16[256,640]{1,0:T(8,128)(2,1)S(1)} %get-tuple-element.127), channel_id=1, source_target_pairs={{8,0},{12,4},{9,1},{13,5},{10,2},{14,6},{11,3},{15,7},{24,16},{28,... | collective-permute-start | bytes 983048 | tf_op jit(solution)/shard_map/ppermute | solution.py:18
  239.9 17.2 %collective-permute-start.21 = (bf16[256,640]{1,0:T(8,128)(2,1)S(1)}, bf16[256,640]{1,0:T(8,128)(2,1)S(1)}, u32[]{:S(2)}, u32[]{:S(2)}) collective-permute-start(bf16[256,640]{1,0:T(8,128)(2,1)S(1)} %get-tuple-element.127), channel_id=1, source_target_pairs={{4,0},{8,4},{12,8},{5,1},{9,5},{13,9},{6,2},{10,6},{14,10},{7,3},{... | collective-permute-start | bytes 983048 | tf_op jit(solution)/shard_map/ppermute | solution.py:18
  241.2 15.8 %collective-permute-start.20 = (bf16[256,640]{1,0:T(8,128)(2,1)S(1)}, bf16[256,640]{1,0:T(8,128)(2,1)S(1)}, u32[]{:S(2)}, u32[]{:S(2)}) collective-permute-start(bf16[256,640]{1,0:T(8,128)(2,1)S(1)} %get-tuple-element.127), channel_id=1, source_target_pairs={{0,4},{4,8},{8,12},{1,5},{5,9},{9,13},{2,6},{6,10},{10,14},{3,7},{... | collective-permute-start | bytes 983048 | tf_op jit(solution)/shard_map/ppermute | solution.py:18
  244.2 12.7 %collective-permute-start.19 = (bf16[256,640]{1,0:T(8,128)(2,1)S(1)}, bf16[256,640]{1,0:T(8,128)(2,1)S(1)}, u32[]{:S(2)}, u32[]{:S(2)}) collective-permute-start(bf16[256,640]{1,0:T(8,128)(2,1)S(1)} %get-tuple-element.127), channel_id=1, source_target_pairs={{0,8},{4,12},{1,9},{5,13},{2,10},{6,14},{3,11},{7,15},{16,24},{20,... | collective-permute-start | bytes 983048 | tf_op jit(solution)/shard_map/ppermute | solution.py:18
  249.9 16.3 %collective-permute-start.34 = (bf16[256,1280]{1,0:T(8,128)(2,1)S(1)}, bf16[256,1280]{1,0:T(8,128)(2,1)S(1)}, u32[]{:S(2)}, u32[]{:S(2)}) collective-permute-start(bf16[256,1280]{1,0:T(8,128)(2,1)S(1)} %fusion.17), channel_id=1, source_target_pairs={{0,16},{1,17},{2,18},{3,19},{4,20},{5,21},{6,22},{7,23},{8,24},{9,... | collective-permute-start | bytes 1966088 | tf_op jit(solution)/shard_map/ppermute | solution.py:18
  267.2 119.2 %copy-start.4 = (bf16[256,1280]{1,0:T(8,128)(2,1)}, bf16[256,1280]{1,0:T(8,128)(2,1)S(1)}, u32[]{:S(2)}) copy-start(bf16[256,1280]{1,0:T(8,128)(2,1)S(1)} %get-tuple-element.178) | copy-start | bytes 1966084
  268.1 19.1 %collective-permute-start.23 = (bf16[256,1280]{1,0:T(8,128)(2,1)S(1)}, bf16[256,1280]{1,0:T(8,128)(2,1)S(1)}, u32[]{:S(2)}, u32[]{:S(2)}) collective-permute-start(bf16[256,1280]{1,0:T(8,128)(2,1)S(1)} %fusion.121), channel_id=1, source_target_pairs={{16,0},{17,1},{18,2},{19,3},{20,4},{21,5},{22,6},{23,7},{24,8},{25... | collective-permute-start | bytes 1966088 | tf_op jit(solution)/shard_map/ppermute | solution.py:18
  291.3 18.6 %collective-permute-start.32 = (bf16[256,640]{1,0:T(8,128)(2,1)S(1)}, bf16[256,640]{1,0:T(8,128)(2,1)S(1)}, u32[]{:S(2)}, u32[]{:S(2)}) collective-permute-start(bf16[256,640]{1,0:T(8,128)(2,1)S(1)} %get-tuple-element.129), channel_id=1, source_target_pairs={{8,0},{12,4},{9,1},{13,5},{10,2},{14,6},{11,3},{15,7},{24,16},{28,... | collective-permute-start | bytes 983048 | tf_op jit(solution)/shard_map/ppermute | solution.py:18
  292.6 17.2 %collective-permute-start.31 = (bf16[256,640]{1,0:T(8,128)(2,1)S(1)}, bf16[256,640]{1,0:T(8,128)(2,1)S(1)}, u32[]{:S(2)}, u32[]{:S(2)}) collective-permute-start(bf16[256,640]{1,0:T(8,128)(2,1)S(1)} %get-tuple-element.129), channel_id=1, source_target_pairs={{4,0},{8,4},{12,8},{5,1},{9,5},{13,9},{6,2},{10,6},{14,10},{7,3},{... | collective-permute-start | bytes 983048 | tf_op jit(solution)/shard_map/ppermute | solution.py:18
  293.9 15.8 %collective-permute-start.30 = (bf16[256,640]{1,0:T(8,128)(2,1)S(1)}, bf16[256,640]{1,0:T(8,128)(2,1)S(1)}, u32[]{:S(2)}, u32[]{:S(2)}) collective-permute-start(bf16[256,640]{1,0:T(8,128)(2,1)S(1)} %get-tuple-element.129), channel_id=1, source_target_pairs={{0,4},{4,8},{8,12},{1,5},{5,9},{9,13},{2,6},{6,10},{10,14},{3,7},{... | collective-permute-start | bytes 983048 | tf_op jit(solution)/shard_map/ppermute | solution.py:18
  296.9 12.7 %collective-permute-start.29 = (bf16[256,640]{1,0:T(8,128)(2,1)S(1)}, bf16[256,640]{1,0:T(8,128)(2,1)S(1)}, u32[]{:S(2)}, u32[]{:S(2)}) collective-permute-start(bf16[256,640]{1,0:T(8,128)(2,1)S(1)} %get-tuple-element.129), channel_id=1, source_target_pairs={{0,8},{4,12},{1,9},{5,13},{2,10},{6,14},{3,11},{7,15},{16,24},{20,... | collective-permute-start | bytes 983048 | tf_op jit(solution)/shard_map/ppermute | solution.py:18
  327.8 18.6 %collective-permute-start.38 = (bf16[256,640]{1,0:T(8,128)(2,1)S(1)}, bf16[256,640]{1,0:T(8,128)(2,1)S(1)}, u32[]{:S(2)}, u32[]{:S(2)}) collective-permute-start(bf16[256,640]{1,0:T(8,128)(2,1)S(1)} %get-tuple-element.215), channel_id=1, source_target_pairs={{8,0},{12,4},{9,1},{13,5},{10,2},{14,6},{11,3},{15,7},{24,16},{28,... | collective-permute-start | bytes 983048 | tf_op jit(solution)/shard_map/ppermute | solution.py:18
  329.1 17.3 %collective-permute-start.37 = (bf16[256,640]{1,0:T(8,128)(2,1)S(1)}, bf16[256,640]{1,0:T(8,128)(2,1)S(1)}, u32[]{:S(2)}, u32[]{:S(2)}) collective-permute-start(bf16[256,640]{1,0:T(8,128)(2,1)S(1)} %get-tuple-element.215), channel_id=1, source_target_pairs={{4,0},{8,4},{12,8},{5,1},{9,5},{13,9},{6,2},{10,6},{14,10},{7,3},{... | collective-permute-start | bytes 983048 | tf_op jit(solution)/shard_map/ppermute | solution.py:18
  330.4 15.8 %collective-permute-start.36 = (bf16[256,640]{1,0:T(8,128)(2,1)S(1)}, bf16[256,640]{1,0:T(8,128)(2,1)S(1)}, u32[]{:S(2)}, u32[]{:S(2)}) collective-permute-start(bf16[256,640]{1,0:T(8,128)(2,1)S(1)} %get-tuple-element.215), channel_id=1, source_target_pairs={{0,4},{4,8},{8,12},{1,5},{5,9},{9,13},{2,6},{6,10},{10,14},{3,7},{... | collective-permute-start | bytes 983048 | tf_op jit(solution)/shard_map/ppermute | solution.py:18
  333.5 12.7 %collective-permute-start.35 = (bf16[256,640]{1,0:T(8,128)(2,1)S(1)}, bf16[256,640]{1,0:T(8,128)(2,1)S(1)}, u32[]{:S(2)}, u32[]{:S(2)}) collective-permute-start(bf16[256,640]{1,0:T(8,128)(2,1)S(1)} %get-tuple-element.215), channel_id=1, source_target_pairs={{0,8},{4,12},{1,9},{5,13},{2,10},{6,14},{3,11},{7,15},{16,24},{20,... | collective-permute-start | bytes 983048 | tf_op jit(solution)/shard_map/ppermute | solution.py:18
  339.4 17.6 %collective-permute-start.33 = (bf16[256,1280]{1,0:T(8,128)(2,1)S(1)}, bf16[256,1280]{1,0:T(8,128)(2,1)S(1)}, u32[]{:S(2)}, u32[]{:S(2)}) collective-permute-start(bf16[256,1280]{1,0:T(8,128)(2,1)S(1)} %fusion.122), channel_id=1, source_target_pairs={{16,0},{17,1},{18,2},{19,3},{20,4},{21,5},{22,6},{23,7},{24,8},{25... | collective-permute-start | bytes 1966088 | tf_op jit(solution)/shard_map/ppermute | solution.py:18
  351.4 71.7 %copy-start.24 = (bf16[256,640]{1,0:T(8,128)(2,1)}, bf16[256,640]{1,0:T(8,128)(2,1)S(1)}, u32[]{:S(2)}) copy-start(bf16[256,640]{1,0:T(8,128)(2,1)S(1)} %get-tuple-element.213) | copy-start | bytes 983044
  361.2 9.7 %collective-permute-start.39 = (bf16[256,640]{1,0:T(8,128)(2,1)S(1)}, bf16[256,640]{1,0:T(8,128)(2,1)S(1)}, u32[]{:S(2)}, u32[]{:S(2)}) collective-permute-start(bf16[256,640]{1,0:T(8,128)(2,1)S(1)} %get-tuple-element.131), channel_id=1, source_target_pairs={{0,8},{4,12},{1,9},{5,13},{2,10},{6,14},{3,11},{7,15},{16,24},{20,... | collective-permute-start | bytes 983048 | tf_op jit(solution)/shard_map/ppermute | solution.py:18
  362.9 8.0 %collective-permute-start.40 = (bf16[256,640]{1,0:T(8,128)(2,1)S(1)}, bf16[256,640]{1,0:T(8,128)(2,1)S(1)}, u32[]{:S(2)}, u32[]{:S(2)}) collective-permute-start(bf16[256,640]{1,0:T(8,128)(2,1)S(1)} %get-tuple-element.131), channel_id=1, source_target_pairs={{0,4},{4,8},{8,12},{1,5},{5,9},{9,13},{2,6},{6,10},{10,14},{3,7},{... | collective-permute-start | bytes 983048 | tf_op jit(solution)/shard_map/ppermute | solution.py:18
  364.3 11.6 %collective-permute-start.42 = (bf16[256,640]{1,0:T(8,128)(2,1)S(1)}, bf16[256,640]{1,0:T(8,128)(2,1)S(1)}, u32[]{:S(2)}, u32[]{:S(2)}) collective-permute-start(bf16[256,640]{1,0:T(8,128)(2,1)S(1)} %get-tuple-element.131), channel_id=1, source_target_pairs={{8,0},{12,4},{9,1},{13,5},{10,2},{14,6},{11,3},{15,7},{24,16},{28,... | collective-permute-start | bytes 983048 | tf_op jit(solution)/shard_map/ppermute | solution.py:18
  365.6 5.5 collective-permute-start.41
  387.3 16.9 %collective-permute-start.43 = (bf16[256,1280]{1,0:T(8,128)(2,1)S(1)}, bf16[256,1280]{1,0:T(8,128)(2,1)S(1)}, u32[]{:S(2)}, u32[]{:S(2)}) collective-permute-start(bf16[256,1280]{1,0:T(8,128)(2,1)S(1)} %fusion.123), channel_id=1, source_target_pairs={{16,0},{17,1},{18,2},{19,3},{20,4},{21,5},{22,6},{23,7},{24,8},{25... | collective-permute-start | bytes 1966088 | tf_op jit(solution)/shard_map/ppermute | solution.py:18
  409.6 43.3 %collective-permute-start.47 = (bf16[256,640]{1,0:T(8,128)(2,1)}, bf16[256,640]{1,0:T(8,128)(2,1)}, u32[]{:S(2)}, u32[]{:S(2)}) collective-permute-start(bf16[256,640]{1,0:T(8,128)(2,1)} %get-tuple-element.133), channel_id=1, source_target_pairs={{8,0},{12,4},{9,1},{13,5},{10,2},{14,6},{11,3},{15,7},{24,16},{28,... | collective-permute-start | bytes 983048 | tf_op jit(solution)/shard_map/ppermute | solution.py:18
  410.9 40.8 %collective-permute-start.46 = (bf16[256,640]{1,0:T(8,128)(2,1)}, bf16[256,640]{1,0:T(8,128)(2,1)}, u32[]{:S(2)}, u32[]{:S(2)}) collective-permute-start(bf16[256,640]{1,0:T(8,128)(2,1)} %get-tuple-element.133), channel_id=1, source_target_pairs={{4,0},{8,4},{12,8},{5,1},{9,5},{13,9},{6,2},{10,6},{14,10},{7,3},{... | collective-permute-start | bytes 983048 | tf_op jit(solution)/shard_map/ppermute | solution.py:18
  412.2 37.3 %collective-permute-start.45 = (bf16[256,640]{1,0:T(8,128)(2,1)}, bf16[256,640]{1,0:T(8,128)(2,1)}, u32[]{:S(2)}, u32[]{:S(2)}) collective-permute-start(bf16[256,640]{1,0:T(8,128)(2,1)} %get-tuple-element.133), channel_id=1, source_target_pairs={{0,4},{4,8},{8,12},{1,5},{5,9},{9,13},{2,6},{6,10},{10,14},{3,7},{... | collective-permute-start | bytes 983048 | tf_op jit(solution)/shard_map/ppermute | solution.py:18
  417.9 30.6 %collective-permute-start.44 = (bf16[256,640]{1,0:T(8,128)(2,1)}, bf16[256,640]{1,0:T(8,128)(2,1)}, u32[]{:S(2)}, u32[]{:S(2)}) collective-permute-start(bf16[256,640]{1,0:T(8,128)(2,1)} %get-tuple-element.133), channel_id=1, source_target_pairs={{0,8},{4,12},{1,9},{5,13},{2,10},{6,14},{3,11},{7,15},{16,24},{20,... | collective-permute-start | bytes 983048 | tf_op jit(solution)/shard_map/ppermute | solution.py:18
  466.5 47.4 %copy-start.84 = (f32[640]{0:T(1024)S(1)}, f32[640]{0:T(1024)}, u32[]{:S(2)}) copy-start(f32[640]{0:T(1024)} %get-tuple-element.39) | copy-start | bytes 7684
  466.5 47.4 %copy-start.51 = (f32[640]{0:T(1024)S(1)}, f32[640]{0:T(1024)}, u32[]{:S(2)}) copy-start(f32[640]{0:T(1024)} %get-tuple-element.134) | copy-start | bytes 7684
  466.5 47.4 %copy-start.54 = (f32[640]{0:T(1024)S(1)}, f32[640]{0:T(1024)}, u32[]{:S(2)}) copy-start(f32[640]{0:T(1024)} %get-tuple-element.138) | copy-start | bytes 7684
  466.5 47.4 %copy-start.56 = (f32[640]{0:T(1024)S(1)}, f32[640]{0:T(1024)}, u32[]{:S(2)}) copy-start(f32[640]{0:T(1024)} %get-tuple-element.140) | copy-start | bytes 7684
  466.5 47.4 %copy-start.3 = (bf16[256,1280]{1,0:T(8,128)(2,1)S(1)}, bf16[256,1280]{1,0:T(8,128)(2,1)}, u32[]{:S(2)}) copy-start(bf16[256,1280]{1,0:T(8,128)(2,1)} %copy-done.2) | copy-start | bytes 1966084
  466.6 47.4 %copy-start.78 = (f32[256]{0:T(256)S(1)}, f32[256]{0:T(256)}, u32[]{:S(2)}) copy-start(f32[256]{0:T(256)} %copy-done.77) | copy-start | bytes 3076
  (132 other events, 1850.9 us)
Sparse Core Ops, SparseCore 0:
  465.2 269.8 all-reduce.4
where the time goes:
time: 762 us; the launch traced here: 755 us
  waiting for transfers between devices  241 us (32%)
  matrix products  139 us (18%)
  starting transfers between devices  121 us (16%)
  blocking collectives  106 us (14%)
  other arithmetic  92 us (12%)
  local copies, waits for them, and re-layouts  38.6 us (5%)
  between operations  18.1 us (2%)
    psum x1, waiting for transfers between devices, shards(): summed = lax.psum(flattened, ('seq', 'dp'))  145 us
    ppermute x48, starting transfers between devices, from_behind(): return lax.ppermute(value, axis, pairs)  121 us
    ppermute x48, waiting for transfers between devices, from_behind(): return lax.ppermute(value, axis, pairs)  96.1 us
    psum x1, blocking collectives, shards(): summed = lax.psum(flattened, ('seq', 'dp'))  64.5 us
    psum x1, blocking collectives, shards(): lax.psum((type_hits, type_tally), ('section', 'seq', 'dp'))  41.4 us
    unnamed x337, local copies, waits for them, and re-layouts  37.1 us
    dot_general x5, matrix products, backward_block(): lax.dot_general(stacked, grad_second_low, contract, preferred_element_typ...  34.3 us
    dot_general x5, matrix products, backward_block(): jnp.dot(grad_first_low, in_weight.T, preferred_element_type=jnp.float32)  25.1 us
  transfers between devices with their start and end apart: 49, of which 16 were waited for; matrix products, arithmetic and copies ran while one was open for 17% of the time, Pallas kernels for 0%

commit v1 on v0

--- a/solution.py
+++ b/solution.py
@@ -1,6 +1,10 @@
+import functools
+
 import jax
 import jax.numpy as jnp
 from jax import lax
+from jax.experimental import pallas as pl
+from jax.experimental.pallas import tpu as pltpu
 from jax.sharding import PartitionSpec as P
 
 KERNEL = 5
@@ -10,6 +14,234 @@
 
 
 EPSILON = 1e-05
+
+
+MESH = pl.DeviceIdType.MESH
+WIDE = 640
+SUBS = 2
+
+def ring_sizes(rows, nodes):
+    units = -(-rows // (nodes * 16))
+    long = -(-units // 2)
+    return [[16 * ((way + i) // SUBS) for i in range(SUBS)] for way in (long, units - long)]
+
+
+def ring_kernel(ny, nz, sizes, w_ref, s_ref, o_ref, t_ref, core_land, *rest):
+    nodes = ny * nz
+    flows = [(way, i) for way in range(2) for i in range(len(sizes[way])) if sizes[way][i]]
+    lands = rest[:len(flows)]
+    small_land, core_send, core_recv, ring_send, ring_recv, back_send, back_recv, small_send, small_recv = rest[len(flows):]
+    s = lax.axis_index("section")
+    q = lax.axis_index("seq")
+    d = lax.axis_index("dp")
+    core = q % 2
+    ypos = q // 2
+    odd = ypos % 2
+    spot = ypos * nz + d + odd * (nz - 1 - 2 * d)
+
+    def at_spot(place):
+        yy = place // nz
+        dd = place % nz
+        dd = dd + (yy % 2) * (nz - 1 - 2 * dd)
+        return (s, yy * 2 + core, dd)
+
+    other_core = (s, q + 1 - 2 * core, d)
+    other_x = (1 - s, q, d)
+    ahead = at_spot((spot + 1) % nodes)
+    behind = at_spot((spot + nodes - 1) % nodes)
+    half = sum(sum(way) for way in sizes) * nodes
+    turn = [1 - 2 * core, 2 * core - 1]
+
+    peers = [other_core]
+    reach = 1
+    while reach < ny:
+        peers.append((s, q + 2 * reach - 4 * reach * ((ypos // reach) % 2), d))
+        reach *= 2
+    reach = 1
+    while reach < nz:
+        peers.append((s, q, d + reach - 2 * reach * ((d // reach) % 2)))
+        reach *= 2
+
+    barrier = pltpu.get_barrier_semaphore()
+    greet = [other_core, other_x, ahead, behind] + peers[1:]
+    for peer in greet:
+        pl.semaphore_signal(barrier, inc=1, device_id=peer, device_id_type=MESH)
+    pl.semaphore_wait(barrier, len(greet))
+
+    first = {}
+    at = 0
+    for way, i in flows:
+        first[way, i] = at
+        at += sizes[way][i] * nodes
+
+    def rows_of(flow, side, shard):
+        way, i = flow
+        return pl.ds(pl.multiple_of(side * half + first[flow] + shard * sizes[way][i], 16), sizes[way][i])
+
+    def shard_at(flow, step):
+        return (spot + 2 * nodes - turn[flow[0]] * step) % nodes
+
+    def next_of(flow):
+        return at_spot((spot + nodes + turn[flow[0]]) % nodes)
+
+    def core_copy(f, shard):
+        flow = flows[f]
+        return pltpu.make_async_remote_copy(
+            src_ref=w_ref.at[rows_of(flow, 1 - core, shard)],
+            dst_ref=core_land.at[rows_of(flow, 0, shard)],
+            send_sem=core_send.at[f, shard], recv_sem=core_recv.at[f, shard],
+            device_id=other_core, device_id_type=MESH)
+
+    def ring_copy(f, step, shard):
+        flow = flows[f]
+        return pltpu.make_async_remote_copy(
+            src_ref=w_ref.at[rows_of(flow, core, shard)],
+            dst_ref=lands[f].at[step],
+            send_sem=ring_send.at[f, step], recv_sem=ring_recv.at[f, step],
+            device_id=next_of(flow), device_id_type=MESH)
+
+    def back_copy(f, step, shard):
+        block = o_ref.at[rows_of(flows[f], core, shard)]
+        return pltpu.make_async_remote_copy(
+            src_ref=block, dst_ref=block,
+            send_sem=ring_send.at[f, nodes - 1 + step], recv_sem=ring_recv.at[f, nodes - 1 + step],
+            device_id=next_of(flows[f]), device_id_type=MESH)
+
+    def over_copy(f, shard):
+        block = o_ref.at[rows_of(flows[f], core, shard)]
+        return pltpu.make_async_remote_copy(
+            src_ref=block, dst_ref=block,
+            send_sem=back_send.at[f, shard], recv_sem=back_recv.at[f, shard],
+            device_id=other_core, device_id_type=MESH)
+
+    def add(f, shard, step, target):
+        flow = flows[f]
+        rows = sizes[flow[0]][flow[1]]
+        here = rows_of(flow, core, shard).start
+        there = rows_of(flow, 0, shard).start
+
+        def body(i, carry):
+            off = pl.multiple_of(i * 16, 16)
+            total = w_ref[pl.ds(here + off, 16)].astype(jnp.float32)
+            total = total + core_land[pl.ds(there + off, 16)].astype(jnp.float32)
+            if step is not None:
+                total = total + lands[f][step, pl.ds(off, 16)].astype(jnp.float32)
+            target[pl.ds(here + off, 16)] = total.astype(target.dtype)
+            return carry
+
+        lax.fori_loop(0, rows // 16, body, 0)
+
+    def to_other_core(step, carry):
+        for f, flow in enumerate(flows):
+            core_copy(f, shard_at(flow, step)).start()
+        return carry
+
+    lax.fori_loop(0, nodes, to_other_core, 0)
+
+    def towards(step, carry):
+        for f, flow in enumerate(flows):
+            shard = shard_at(flow, step)
+            core_copy(f, shard).wait_recv()
+            if carry is None:
+                add(f, shard, None, w_ref)
+            else:
+                ring_copy(f, step - 1, shard).wait_recv()
+                add(f, shard, step - 1, w_ref)
+            ring_copy(f, step, shard).start()
+        return carry
+
+    towards(0, None)
+    count = s_ref.shape[0]
+
+    def held(k):
+        return s_ref if k == 0 else small_land.at[2 * k - 1]
+
+    def small_copy(k):
+        last = k == len(peers)
+        return pltpu.make_async_remote_copy(
+            src_ref=held(k), dst_ref=t_ref.at[pl.ds(count, count)] if last else small_land.at[2 * k],
+            send_sem=small_send.at[k], recv_sem=small_recv.at[k],
+            device_id=other_x if last else peers[k], device_id_type=MESH)
+
+    def small_step(k):
+        if 0 < k <= len(peers):
+            small_copy(k - 1).wait_recv()
+            small_land[2 * k - 1] = held(k - 1)[...] + small_land[2 * k - 2]
+        if k <= len(peers):
+            small_copy(k).start()
+        if k == len(peers):
+            t_ref[pl.ds(0, count)] = held(k)[...]
+
+    small_step(0)
+    for k in range(1, len(peers) + 1):
+        if k < nodes - 1:
+            towards(k, 0)
+        small_step(k)
+    lax.fori_loop(min(len(peers) + 1, nodes - 1), nodes - 1, towards, 0)
+    for f, flow in enumerate(flows):
+        shard = shard_at(flow, nodes - 1)
+        core_copy(f, shard).wait_recv()
+        ring_copy(f, nodes - 2, shard).wait_recv()
+        add(f, shard, nodes - 2, o_ref)
+        back_copy(f, 0, shard).start()
+        over_copy(f, shard).start()
+
+    def back(step, carry):
+        for f, flow in enumerate(flows):
+            shard = shard_at(flow, nodes - 1 + step)
+            back_copy(f, step - 1, shard).wait_recv()
+            back_copy(f, step, shard).start()
+            over_copy(f, shard).start()
+        return carry
+
+    lax.fori_loop(1, nodes - 1, back, 0)
+    for f, flow in enumerate(flows):
+        shard = shard_at(flow, 2 * nodes - 2)
+        back_copy(f, nodes - 2, shard).wait_recv()
+        over_copy(f, shard).start()
+
+    def settle(step, carry):
+        for f, flow in enumerate(flows):
+            core_copy(f, step).wait_send()
+            over_copy(f, step).wait()
+        return carry
+
+    def settle_ring(step, carry):
+        for f, flow in enumerate(flows):
+            ring_copy(f, step, 0).wait_send()
+            back_copy(f, step, 0).wait_send()
+        return carry
+
+    lax.fori_loop(0, nodes, settle, 0)
+    lax.fori_loop(0, nodes - 1, settle_ring, 0)
+    for k in range(len(peers) + 1):
+        small_copy(k).wait_send()
+    small_copy(len(peers)).wait_recv()
+
+
+def sum_everywhere(big, small, ny, nz, cid=1):
+    rows = big.shape[0]
+    nodes = ny * nz
+    sizes = ring_sizes(rows // 2, nodes)
+    flows = [(w, i) for w in range(2) for i in range(len(sizes[w])) if sizes[w][i]]
+    half = sum(map(sum, sizes)) * nodes
+    assert rows == 2 * half, (rows, half, sizes)
+    n = len(flows)
+    return pl.pallas_call(
+        functools.partial(ring_kernel, ny, nz, sizes),
+        out_shape=(jax.ShapeDtypeStruct(big.shape, big.dtype),
+                   jax.ShapeDtypeStruct((2 * small.shape[0], small.shape[1]), small.dtype)),
+        in_specs=[pl.BlockSpec(memory_space=pltpu.VMEM)] * 2,
+        out_specs=[pl.BlockSpec(memory_space=pltpu.VMEM)] * 2,
+        scratch_shapes=[pltpu.VMEM((half, WIDE), big.dtype)]
+        + [pltpu.VMEM((nodes - 1, sizes[w][i], WIDE), big.dtype) for w, i in flows]
+        + [pltpu.VMEM((16,) + small.shape, small.dtype)]
+        + [pltpu.SemaphoreType.DMA((n, nodes))] * 2
+        + [pltpu.SemaphoreType.DMA((n, 2 * nodes - 2))] * 2
+        + [pltpu.SemaphoreType.DMA((n, nodes))] * 2
+        + [pltpu.SemaphoreType.DMA((8,))] * 2,
+        compiler_params=pltpu.CompilerParams(collective_id=cid, has_side_effects=True, vmem_limit_bytes=56 << 20),
+    )(big, small)
 
 
 def from_behind(value, axis, by):
@@ -287,8 +519,6 @@
     ends_grad = jnp.stack(input_grads[1:], axis=0)
     ends_out = jnp.stack(outputs[1:], axis=0)
     boundary_out = jnp.where(leading_section, ends_grad, ends_out)[None]
-    flattened = tuple((total.reshape(1, -1) for total in grad_totals))
-    summed = lax.psum(flattened, ("seq", "dp"))
     (
         grad_first_gain,
         grad_first_shift,
@@ -302,8 +532,45 @@
         grad_third_shift,
         grad_out_weight,
         grad_out_bias,
-    ) = tuple((total.reshape((1,) + item.shape) for total, item in zip(summed, weights)))
-    type_hits, type_tally = lax.psum((type_hits, type_tally), ("section", "seq", "dp"))
+    ) = grad_totals
+    hidden = in_bias.shape[1]
+    ny, nz = lax.axis_size("seq") // 2, lax.axis_size("dp")
+    taps = conv_weight.shape[1]
+    count = (taps + 4) * hidden
+    spare = 2 * ny * nz * sum(map(sum, ring_sizes(count // 2, ny * nz))) - count
+    big = jnp.concatenate(
+        [
+            grad_in_weight,
+            grad_conv_weight.reshape(taps * hidden, hidden),
+            grad_out_weight[:, :hidden],
+            grad_out_weight[:, hidden:],
+            jnp.zeros((spare, hidden), jnp.float32),
+        ]
+    ).astype(jnp.bfloat16)
+    small = jnp.stack(
+        [
+            grad_first_gain,
+            grad_first_shift,
+            grad_out_bias,
+            jnp.concatenate([grad_in_bias, grad_second_gain]),
+            jnp.concatenate([grad_second_shift, grad_conv_bias]),
+            jnp.concatenate([grad_third_gain, grad_third_shift]),
+            jnp.pad(type_hits, (0, width - VOCAB)),
+            jnp.pad(type_tally, (0, width - VOCAB)),
+        ]
+    )
+    big, small = sum_everywhere(big, small, ny, nz)
+    big = big.astype(jnp.float32)
+    grad_in_weight = big[None, :width]
+    grad_conv_weight = big[width : width + taps * hidden].reshape(conv_weight.shape)
+    at = width + taps * hidden
+    grad_out_weight = jnp.concatenate([big[at : at + hidden], big[at + hidden : at + 2 * hidden]], axis=1)[None]
+    grad_first_gain, grad_first_shift, grad_out_bias = small[0:1], small[1:2], small[2:3]
+    grad_in_bias, grad_second_gain = small[3:4, :hidden], small[3:4, hidden:]
+    grad_second_shift, grad_conv_bias = small[4:5, :hidden], small[4:5, hidden:]
+    grad_third_gain, grad_third_shift = small[5:6, :hidden], small[5:6, hidden:]
+    type_hits = small[6, :VOCAB] + small[14, :VOCAB]
+    type_tally = small[7, :VOCAB] + small[15, :VOCAB]
     type_scores = type_hits / jnp.maximum(type_tally, 1.0)
     type_counts = type_tally.astype(jnp.int32)
     return (

time: 762 us -> 575 us (0.75)
  waiting for transfers between devices: 241 us -> 107 us
  blocking collectives: 106 us -> 0 us
  Pallas kernels: 0 us -> 92.9 us
  matrix products: 139 us -> 117 us
  between operations: 18.1 us -> 4.18 us
    psum x1 -> x0, waiting for transfers between devices: 145 us -> none  [shards(): summed = lax.psum(flattened, ('seq', 'dp'))]
    psum x2 -> x0, blocking collectives: 106 us -> none  [the longest x1 64.5 us: shards(): summed = lax.psum(flattened, ('seq', 'dp'))]
    pallas_call x0 -> x1, Pallas kernels: none -> 92.9 us  [sum_everywhere(): pl.pallas_call(functools.partial(ring_kernel, ny, nz, sizes), out_shape=(...]
    unnamed x337 -> x194, local copies, waits for them, and re-layouts: 37.1 us -> 21.4 us
    slice x0 -> x4, local copies, waits for them, and re-layouts: none -> 12.6 us  [the longest x1 6.16 us: shards(): big[width:width + taps * hidden].reshape(conv_weight.shape)]
    ppermute x48, waiting for transfers between devices: 96.1 us -> 107 us  [from_behind(): return lax.ppermute(value, axis, pairs)]
    dot_general x5, matrix products: 17.2 us -> 6.54 us  [backward_block(): lax.dot_general(third_act, grad_out, contract, preferred_element_type=jnp...]
  transfers between devices with their start and end apart: 49 -> 48, of which waited for: 16 -> 16; matrix products, arithmetic and copies ran while one was open for 17% -> 13% of each run, Pallas kernels for 0% -> 0%
where the time goes in v1:
time: 575 us; the launch traced here: 570 us
  starting transfers between devices  120 us (21%)
  matrix products  117 us (20%)
  waiting for transfers between devices  107 us (19%)
  Pallas kernels  92.9 us (16%)
  other arithmetic  88.7 us (15%)
  local copies, waits for them, and re-layouts  39.8 us (7%)
    ppermute x48, starting transfers between devices, from_behind(): return lax.ppermute(value, axis, pairs)  120 us
    ppermute x48, waiting for transfers between devices, from_behind(): return lax.ppermute(value, axis, pairs)  107 us
    pallas_call x1, Pallas kernels, sum_everywhere(): pl.pallas_call(functools.partial(ring_kernel, ny, nz, sizes), out_shape=(...  92.9 us
    dot_general x5, matrix products, backward_block(): lax.dot_general(stacked, grad_second_low, contract, preferred_element_typ...  32.1 us
    dot_general x5, matrix products, backward_block(): jnp.dot(grad_first_low, in_weight.T, preferred_element_type=jnp.float32)  23.5 us
    unnamed x194, local copies, waits for them, and re-layouts  21.4 us
    reduce_sum x12, other arithmetic, norm_act(): average = jnp.mean(values, axis=-1, keepdims=True)  20.5 us
    dot_general x5, matrix products, backward_block(): jnp.dot(back_stacked, conv_back, preferred_element_type=jnp.float32)  16.3 us
  transfers between devices with their start and end apart: 48, of which 16 were waited for; matrix products, arithmetic and copies ran while one was open for 13% of the time, Pallas kernels for 0%

profile of v1, /device:TPU:0, one launch (start us, length us, event | category | flops | bytes accessed | tf_op | source)
XLA Modules:
  0.0 569.6 jit_solution(6709840239582988910)
XLA Ops:
  5.9 5.0 fusion.724
  15.5 3.8 collective-permute-start.1
  19.3 6.0 %collective-permute-start = (bf16[256,640]{1,0:T(8,128)(2,1)S(1)}, bf16[256,640]{1,0:T(8,128)(2,1)}, u32[]{:S(2)}, u32[]{:S(2)}) collective-permute-start(bf16[256,640]{1,0:T(8,128)(2,1)S(1)} %fusion.304), channel_id=1, source_target_pairs={{0,8},{4,12},{1,9},{5,13},{2,10},{6,14},{3,11},{7,15},{16,24},{20,... | collective-permute-start | bytes 983048 | tf_op jit(solution)/shard_map/ppermute | solution.py:250
  28.7 7.9 %copy.33 = bf16[1,5,640,640]{2,3,1,0:T(8,128)(2,1)} copy(bf16[1,5,640,640]{3,2,1,0:T(8,128)(2,1)} %param.28) | data formatting | bytes 8192000 | tf_op args[11]
  48.7 4.7 collective-permute-start.4
  54.6 11.9 %collective-permute-done.4 = bf16[256,1280]{1,0:T(8,128)(2,1)S(1)} collective-permute-done((bf16[256,1280]{1,0:T(8,128)(2,1)S(1)}, bf16[256,1280]{1,0:T(8,128)(2,1)S(1)}, u32[]{:S(2)}, u32[]{:S(2)}) %collective-permute-start.4) | collective-permute-done | bytes 655392 | tf_op jit(solution)/shard_map/ppermute | solution.py:250
  67.1 3.5 fusion.111
  75.9 3.1 collective-permute-start.6
  78.9 4.6 collective-permute-start.5
  83.7 7.9 %collective-permute-done.5 = bf16[256,640]{1,0:T(8,128)(2,1)S(1)} collective-permute-done((bf16[256,640]{1,0:T(8,128)(2,1)S(1)}, bf16[256,640]{1,0:T(8,128)(2,1)S(1)}, u32[]{:S(2)}, u32[]{:S(2)}) %collective-permute-start.5) | collective-permute-done | bytes 327712 | tf_op jit(solution)/shard_map/ppermute | solution.py:250
  97.2 4.4 collective-permute-start.14
  101.8 2.9 multiply_reduce_fusion.19
  108.4 3.1 collective-permute-start.10
  111.4 4.8 collective-permute-start.9
  116.2 4.7 fusion.60
  120.9 2.4 convolution_select_fusion.4
  126.4 3.7 multiply_reduce_fusion.24
  132.7 5.0 multiply_reduce_fusion.4
  138.1 3.9 fusion.102
  147.3 3.1 collective-permute-start.16
  150.4 4.5 collective-permute-start.15
  155.2 7.9 %collective-permute-done.15 = bf16[256,640]{1,0:T(8,128)(2,1)S(1)} collective-permute-done((bf16[256,640]{1,0:T(8,128)(2,1)S(1)}, bf16[256,640]{1,0:T(8,128)(2,1)S(1)}, u32[]{:S(2)}, u32[]{:S(2)}) %collective-permute-start.15) | collective-permute-done | bytes 327712 | tf_op jit(solution)/shard_map/ppermute | solution.py:250
  170.4 14.5 %collective-permute-done.24 = bf16[256,1280]{1,0:T(8,128)(2,1)S(1)} collective-permute-done((bf16[256,1280]{1,0:T(8,128)(2,1)S(1)}, bf16[256,1280]{1,0:T(8,128)(2,1)S(1)}, u32[]{:S(2)}, u32[]{:S(2)}) %collective-permute-start.24) | collective-permute-done | bytes 655392 | tf_op jit(solution)/shard_map/ppermute | solution.py:250
  184.9 4.8 fusion.296
  190.6 3.5 fusion.93
  199.4 3.1 collective-permute-start.26
  202.4 4.6 collective-permute-start.25
  209.0 6.1 %collective-permute-done.25 = bf16[256,640]{1,0:T(8,128)(2,1)S(1)} collective-permute-done((bf16[256,640]{1,0:T(8,128)(2,1)S(1)}, bf16[256,640]{1,0:T(8,128)(2,1)S(1)}, u32[]{:S(2)}, u32[]{:S(2)}) %collective-permute-start.25) | collective-permute-done | bytes 327712 | tf_op jit(solution)/shard_map/ppermute | solution.py:250
  218.0 7.1 %collective-permute-done.13 = bf16[256,1280]{1,0:T(8,128)(2,1)S(1)} collective-permute-done((bf16[256,1280]{1,0:T(8,128)(2,1)S(1)}, bf16[256,1280]{1,0:T(8,128)(2,1)S(1)}, u32[]{:S(2)}, u32[]{:S(2)}) %collective-permute-start.13) | collective-permute-done | bytes 655392 | tf_op jit(solution)/shard_map/ppermute | solution.py:250
  225.3 2.3 multiply_reduce_fusion.18
  232.4 3.1 collective-permute-start.20
  235.5 4.6 collective-permute-start.19
  243.0 4.7 fusion.58
  249.2 3.1 multiply_reduce_fusion.23
  252.8 3.8 fusion.146
  261.0 16.7 %collective-permute-done.23 = bf16[256,1280]{1,0:T(8,128)(2,1)S(1)} collective-permute-done((bf16[256,1280]{1,0:T(8,128)(2,1)S(1)}, bf16[256,1280]{1,0:T(8,128)(2,1)S(1)}, u32[]{:S(2)}, u32[]{:S(2)}) %collective-permute-start.23) | collective-permute-done | bytes 655392 | tf_op jit(solution)/shard_map/ppermute | solution.py:250
  283.3 3.1 collective-permute-start.30
  286.3 4.6 collective-permute-start.29
  290.9 4.7 fusion.56
  296.3 2.7 collective-permute-done.29
  300.1 3.2 multiply_reduce_fusion.22
  303.7 4.6 multiply_reduce_fusion.2
  308.7 4.1 fusion.698
  318.2 3.1 collective-permute-start.36
  321.3 4.5 collective-permute-start.35
  329.9 4.1 collective-permute-done.35
  340.7 4.1 collective-permute-done.33
  353.7 3.8 collective-permute-done.39
  357.8 4.8 collective-permute-done.42
  363.4 3.2 multiply_reduce_fusion.21
  367.1 4.4 multiply_reduce_fusion.1
  373.8 4.9 fusion.54
  379.4 9.9 %collective-permute-done.43 = bf16[256,1280]{1,0:T(8,128)(2,1)S(1)} collective-permute-done((bf16[256,1280]{1,0:T(8,128)(2,1)S(1)}, bf16[256,1280]{1,0:T(8,128)(2,1)S(1)}, u32[]{:S(2)}, u32[]{:S(2)}) %collective-permute-start.43) | collective-permute-done | bytes 655392 | tf_op jit(solution)/shard_map/ppermute | solution.py:250
  395.2 5.0 collective-permute-start.45
  400.1 3.7 collective-permute-start.44
  406.9 5.0 collective-permute-done.44
  413.5 3.2 multiply_reduce_fusion.20
  418.3 5.5 multiply_reduce_fusion
  426.0 13.0 %fusion = bf16[5888,640]{1,0:T(8,128)(2,1)} fusion(bf16[5888,640]{1,0:T(8,128)(2,1)} %fusion.11, bf16[256,640]{1,0:T(8,128)(2,1)S(1)} %get-tuple-element.115, f32[3200,640]{1,0:T(8,128)} %fusion.54, f32[3200,640]{1,0:T(8,128)} %fusion.56, f32[3200,640]{1,0:T(8,128)} %fusion.58, f32[3200,640]{1,0:T(8,128)} %fusion.60, pred[]{:T(512)S(6)} %and.444, ...), kind=kOutput, calls=%fused_computation.1 | convolution fusion | flops 1069875200 | bytes 40468488 | tf_op jit(solution)/shard_map/dot_general | solution.py:374
  443.6 92.9 %shard_map.280 = (bf16[5888,640]{1,0:T(8,128)(2,1)}, f32[16,1280]{1,0:T(8,128)}) custom-call(bf16[5888,640]{1,0:T(8,128)(2,1)} %constant_dynamic-update-slice_fusion.50.w_ref, f32[8,1280]{1,0:T(8,128)} %stack.66.s_ref), custom_call_target="tpu_custom_call" | custom-call | tf_op jit(solution)/shard_map/pallas_call | solution.py:230
  540.7 3.5 fusion.721
  544.1 6.2 %slice.153 = f32[3200,640]{1,0:T(8,128)} slice(bf16[5888,640]{1,0:T(8,128)(2,1)} %get-tuple-element.18), slice={[1280:4480], [0:640]} | slice | bytes 16384000 | tf_op jit(solution)/shard_map/slice | solution.py:565
  550.3 6.3 %convert_element_type.590 = f32[5888,640]{1,0:T(8,128)} convert(bf16[5888,640]{1,0:T(8,128)(2,1)S(1)} %bitcast.348) | non-fusion elementwise | flops 3768320 | bytes 22609920 | tf_op jit(solution)/shard_map/convert_element_type | solution.py:563
  558.5 4.0 slice_bitcast_fusion
  (604 shorter events, 152.8 us)
Async XLA Ops:
  10.9 14.4 %copy-start.48 = (f32[1,640]{1,0:T(1,128)S(1)}, f32[1,640]{1,0:T(1,128)}, u32[]{:S(2)}) copy-start(f32[1,640]{1,0:T(1,128)} %param.30) | copy-start | bytes 7684
  10.9 14.4 %copy-start.49 = (f32[1,640]{1,0:T(1,128)S(1)}, f32[1,640]{1,0:T(1,128)}, u32[]{:S(2)}) copy-start(f32[1,640]{1,0:T(1,128)} %param.31) | copy-start | bytes 7684
  11.0 14.5 %copy-start.50 = (f32[1,640]{1,0:T(1,128)S(1)}, f32[1,640]{1,0:T(1,128)}, u32[]{:S(2)}) copy-start(f32[1,640]{1,0:T(1,128)} %param.29) | copy-start | bytes 7684
  11.0 14.5 %copy-start.39 = (f32[1,1280]{1,0:T(1,128)S(1)}, f32[1,1280]{1,0:T(1,128)}, u32[]{:S(2)}) copy-start(f32[1,1280]{1,0:T(1,128)} %param.33) | copy-start | bytes 15364
  12.9 29.2 %collective-permute-start.3 = (bf16[256,640]{1,0:T(8,128)(2,1)S(1)}, bf16[256,640]{1,0:T(8,128)(2,1)S(1)}, u32[]{:S(2)}, u32[]{:S(2)}) collective-permute-start(bf16[256,640]{1,0:T(8,128)(2,1)S(1)} %fusion.304), channel_id=1, source_target_pairs={{8,0},{12,4},{9,1},{13,5},{10,2},{14,6},{11,3},{15,7},{24,16},{28,... | collective-permute-start | bytes 983048 | tf_op jit(solution)/shard_map/ppermute | solution.py:250
  14.2 26.8 %collective-permute-start.2 = (bf16[256,640]{1,0:T(8,128)(2,1)S(1)}, bf16[256,640]{1,0:T(8,128)(2,1)}, u32[]{:S(2)}, u32[]{:S(2)}) collective-permute-start(bf16[256,640]{1,0:T(8,128)(2,1)S(1)} %fusion.304), channel_id=1, source_target_pairs={{4,0},{8,4},{12,8},{5,1},{9,5},{13,9},{6,2},{10,6},{14,10},{7,3},{... | collective-permute-start | bytes 983048 | tf_op jit(solution)/shard_map/ppermute | solution.py:250
  15.5 22.8 %collective-permute-start.1 = (bf16[256,640]{1,0:T(8,128)(2,1)S(1)}, bf16[256,640]{1,0:T(8,128)(2,1)}, u32[]{:S(2)}, u32[]{:S(2)}) collective-permute-start(bf16[256,640]{1,0:T(8,128)(2,1)S(1)} %fusion.304), channel_id=1, source_target_pairs={{0,4},{4,8},{8,12},{1,5},{5,9},{9,13},{2,6},{6,10},{10,14},{3,7},{... | collective-permute-start | bytes 983048 | tf_op jit(solution)/shard_map/ppermute | solution.py:250
  19.3 18.0 %collective-permute-start = (bf16[256,640]{1,0:T(8,128)(2,1)S(1)}, bf16[256,640]{1,0:T(8,128)(2,1)}, u32[]{:S(2)}, u32[]{:S(2)}) collective-permute-start(bf16[256,640]{1,0:T(8,128)(2,1)S(1)} %fusion.304), channel_id=1, source_target_pairs={{0,8},{4,12},{1,9},{5,13},{2,10},{6,14},{3,11},{7,15},{16,24},{20,... | collective-permute-start | bytes 983048 | tf_op jit(solution)/shard_map/ppermute | solution.py:250
  28.7 7.9 %copy-start.35 = (s32[4,256]{1,0:T(4,128)S(1)}, s32[4,256]{1,0:T(4,128)}, u32[]{:S(2)}) copy-start(s32[4,256]{1,0:T(4,128)} %param.20) | copy-start | bytes 12292
  28.7 7.9 %copy-start.36 = (s32[4,256]{1,0:T(4,128)S(1)}, s32[4,256]{1,0:T(4,128)}, u32[]{:S(2)}) copy-start(s32[4,256]{1,0:T(4,128)} %param.19) | copy-start | bytes 12292
  48.0 72.9 %copy-start.11 = (bf16[256,640]{1,0:T(8,128)(2,1)}, bf16[256,640]{1,0:T(8,128)(2,1)S(1)}, u32[]{:S(2)}) copy-start(bf16[256,640]{1,0:T(8,128)(2,1)S(1)} %fusion.308) | copy-start | bytes 983044
  48.7 17.8 %collective-permute-start.4 = (bf16[256,1280]{1,0:T(8,128)(2,1)S(1)}, bf16[256,1280]{1,0:T(8,128)(2,1)S(1)}, u32[]{:S(2)}, u32[]{:S(2)}) collective-permute-start(bf16[256,1280]{1,0:T(8,128)(2,1)S(1)} %fusion.21), channel_id=1, source_target_pairs={{0,16},{1,17},{2,18},{3,19},{4,20},{5,21},{6,22},{7,23},{8,24},{9,... | collective-permute-start | bytes 1966088 | tf_op jit(solution)/shard_map/ppermute | solution.py:250
  73.3 18.6 %collective-permute-start.8 = (bf16[256,640]{1,0:T(8,128)(2,1)S(1)}, bf16[256,640]{1,0:T(8,128)(2,1)S(1)}, u32[]{:S(2)}, u32[]{:S(2)}) collective-permute-start(bf16[256,640]{1,0:T(8,128)(2,1)S(1)} %get-tuple-element.215), channel_id=1, source_target_pairs={{8,0},{12,4},{9,1},{13,5},{10,2},{14,6},{11,3},{15,7},{24,16},{28,... | collective-permute-start | bytes 983048 | tf_op jit(solution)/shard_map/ppermute | solution.py:250
  74.6 17.2 %collective-permute-start.7 = (bf16[256,640]{1,0:T(8,128)(2,1)S(1)}, bf16[256,640]{1,0:T(8,128)(2,1)S(1)}, u32[]{:S(2)}, u32[]{:S(2)}) collective-permute-start(bf16[256,640]{1,0:T(8,128)(2,1)S(1)} %get-tuple-element.215), channel_id=1, source_target_pairs={{4,0},{8,4},{12,8},{5,1},{9,5},{13,9},{6,2},{10,6},{14,10},{7,3},{... | collective-permute-start | bytes 983048 | tf_op jit(solution)/shard_map/ppermute | solution.py:250
  75.9 15.8 %collective-permute-start.6 = (bf16[256,640]{1,0:T(8,128)(2,1)S(1)}, bf16[256,640]{1,0:T(8,128)(2,1)S(1)}, u32[]{:S(2)}, u32[]{:S(2)}) collective-permute-start(bf16[256,640]{1,0:T(8,128)(2,1)S(1)} %get-tuple-element.215), channel_id=1, source_target_pairs={{0,4},{4,8},{8,12},{1,5},{5,9},{9,13},{2,6},{6,10},{10,14},{3,7},{... | collective-permute-start | bytes 983048 | tf_op jit(solution)/shard_map/ppermute | solution.py:250
  78.9 12.7 %collective-permute-start.5 = (bf16[256,640]{1,0:T(8,128)(2,1)S(1)}, bf16[256,640]{1,0:T(8,128)(2,1)S(1)}, u32[]{:S(2)}, u32[]{:S(2)}) collective-permute-start(bf16[256,640]{1,0:T(8,128)(2,1)S(1)} %get-tuple-element.215), channel_id=1, source_target_pairs={{0,8},{4,12},{1,9},{5,13},{2,10},{6,14},{3,11},{7,15},{16,24},{20,... | collective-permute-start | bytes 983048 | tf_op jit(solution)/shard_map/ppermute | solution.py:250
  96.8 7.9 %copy-start.13 = (bf16[256,1280]{1,0:T(8,128)(2,1)}, bf16[256,1280]{1,0:T(8,128)(2,1)S(1)}, u32[]{:S(2)}) copy-start(bf16[256,1280]{1,0:T(8,128)(2,1)S(1)} %fusion.17) | copy-start | bytes 1966084
  97.2 34.0 %collective-permute-start.14 = (bf16[256,1280]{1,0:T(8,128)(2,1)S(1)}, bf16[256,1280]{1,0:T(8,128)(2,1)S(1)}, u32[]{:S(2)}, u32[]{:S(2)}) collective-permute-start(bf16[256,1280]{1,0:T(8,128)(2,1)S(1)} %fusion.17), channel_id=1, source_target_pairs={{0,16},{1,17},{2,18},{3,19},{4,20},{5,21},{6,22},{7,23},{8,24},{9,... | collective-permute-start | bytes 1966088 | tf_op jit(solution)/shard_map/ppermute | solution.py:250
  105.8 18.6 %collective-permute-start.12 = (bf16[256,640]{1,0:T(8,128)(2,1)S(1)}, bf16[256,640]{1,0:T(8,128)(2,1)S(1)}, u32[]{:S(2)}, u32[]{:S(2)}) collective-permute-start(bf16[256,640]{1,0:T(8,128)(2,1)S(1)} %get-tuple-element.107), channel_id=1, source_target_pairs={{8,0},{12,4},{9,1},{13,5},{10,2},{14,6},{11,3},{15,7},{24,16},{28,... | collective-permute-start | bytes 983048 | tf_op jit(solution)/shard_map/ppermute | solution.py:250
  107.1 17.2 %collective-permute-start.11 = (bf16[256,640]{1,0:T(8,128)(2,1)S(1)}, bf16[256,640]{1,0:T(8,128)(2,1)S(1)}, u32[]{:S(2)}, u32[]{:S(2)}) collective-permute-start(bf16[256,640]{1,0:T(8,128)(2,1)S(1)} %get-tuple-element.107), channel_id=1, source_target_pairs={{4,0},{8,4},{12,8},{5,1},{9,5},{13,9},{6,2},{10,6},{14,10},{7,3},{... | collective-permute-start | bytes 983048 | tf_op jit(solution)/shard_map/ppermute | solution.py:250
  108.4 15.8 %collective-permute-start.10 = (bf16[256,640]{1,0:T(8,128)(2,1)S(1)}, bf16[256,640]{1,0:T(8,128)(2,1)S(1)}, u32[]{:S(2)}, u32[]{:S(2)}) collective-permute-start(bf16[256,640]{1,0:T(8,128)(2,1)S(1)} %get-tuple-element.107), channel_id=1, source_target_pairs={{0,4},{4,8},{8,12},{1,5},{5,9},{9,13},{2,6},{6,10},{10,14},{3,7},{... | collective-permute-start | bytes 983048 | tf_op jit(solution)/shard_map/ppermute | solution.py:250
  111.4 12.7 %collective-permute-start.9 = (bf16[256,640]{1,0:T(8,128)(2,1)S(1)}, bf16[256,640]{1,0:T(8,128)(2,1)S(1)}, u32[]{:S(2)}, u32[]{:S(2)}) collective-permute-start(bf16[256,640]{1,0:T(8,128)(2,1)S(1)} %get-tuple-element.107), channel_id=1, source_target_pairs={{0,8},{4,12},{1,9},{5,13},{2,10},{6,14},{3,11},{7,15},{16,24},{20,... | collective-permute-start | bytes 983048 | tf_op jit(solution)/shard_map/ppermute | solution.py:250
  144.7 18.6 %collective-permute-start.18 = (bf16[256,640]{1,0:T(8,128)(2,1)S(1)}, bf16[256,640]{1,0:T(8,128)(2,1)S(1)}, u32[]{:S(2)}, u32[]{:S(2)}) collective-permute-start(bf16[256,640]{1,0:T(8,128)(2,1)S(1)} %get-tuple-element.213), channel_id=1, source_target_pairs={{8,0},{12,4},{9,1},{13,5},{10,2},{14,6},{11,3},{15,7},{24,16},{28,... | collective-permute-start | bytes 983048 | tf_op jit(solution)/shard_map/ppermute | solution.py:250
  146.0 17.2 %collective-permute-start.17 = (bf16[256,640]{1,0:T(8,128)(2,1)S(1)}, bf16[256,640]{1,0:T(8,128)(2,1)S(1)}, u32[]{:S(2)}, u32[]{:S(2)}) collective-permute-start(bf16[256,640]{1,0:T(8,128)(2,1)S(1)} %get-tuple-element.213), channel_id=1, source_target_pairs={{4,0},{8,4},{12,8},{5,1},{9,5},{13,9},{6,2},{10,6},{14,10},{7,3},{... | collective-permute-start | bytes 983048 | tf_op jit(solution)/shard_map/ppermute | solution.py:250
  147.3 15.8 %collective-permute-start.16 = (bf16[256,640]{1,0:T(8,128)(2,1)S(1)}, bf16[256,640]{1,0:T(8,128)(2,1)S(1)}, u32[]{:S(2)}, u32[]{:S(2)}) collective-permute-start(bf16[256,640]{1,0:T(8,128)(2,1)S(1)} %get-tuple-element.213), channel_id=1, source_target_pairs={{0,4},{4,8},{8,12},{1,5},{5,9},{9,13},{2,6},{6,10},{10,14},{3,7},{... | collective-permute-start | bytes 983048 | tf_op jit(solution)/shard_map/ppermute | solution.py:250
  150.4 12.7 %collective-permute-start.15 = (bf16[256,640]{1,0:T(8,128)(2,1)S(1)}, bf16[256,640]{1,0:T(8,128)(2,1)S(1)}, u32[]{:S(2)}, u32[]{:S(2)}) collective-permute-start(bf16[256,640]{1,0:T(8,128)(2,1)S(1)} %get-tuple-element.213), channel_id=1, source_target_pairs={{0,8},{4,12},{1,9},{5,13},{2,10},{6,14},{3,11},{7,15},{16,24},{20,... | collective-permute-start | bytes 983048 | tf_op jit(solution)/shard_map/ppermute | solution.py:250
  168.2 21.5 %copy-start.15 = (bf16[256,1280]{1,0:T(8,128)(2,1)}, bf16[256,1280]{1,0:T(8,128)(2,1)S(1)}, u32[]{:S(2)}) copy-start(bf16[256,1280]{1,0:T(8,128)(2,1)S(1)} %fusion.18) | copy-start | bytes 1966084
  168.6 16.3 %collective-permute-start.24 = (bf16[256,1280]{1,0:T(8,128)(2,1)S(1)}, bf16[256,1280]{1,0:T(8,128)(2,1)S(1)}, u32[]{:S(2)}, u32[]{:S(2)}) collective-permute-start(bf16[256,1280]{1,0:T(8,128)(2,1)S(1)} %fusion.18), channel_id=1, source_target_pairs={{0,16},{1,17},{2,18},{3,19},{4,20},{5,21},{6,22},{7,23},{8,24},{9,... | collective-permute-start | bytes 1966088 | tf_op jit(solution)/shard_map/ppermute | solution.py:250
  196.8 18.6 %collective-permute-start.28 = (bf16[256,640]{1,0:T(8,128)(2,1)S(1)}, bf16[256,640]{1,0:T(8,128)(2,1)S(1)}, u32[]{:S(2)}, u32[]{:S(2)}) collective-permute-start(bf16[256,640]{1,0:T(8,128)(2,1)S(1)} %get-tuple-element.210), channel_id=1, source_target_pairs={{8,0},{12,4},{9,1},{13,5},{10,2},{14,6},{11,3},{15,7},{24,16},{28,... | collective-permute-start | bytes 983048 | tf_op jit(solution)/shard_map/ppermute | solution.py:250
  198.1 17.2 %collective-permute-start.27 = (bf16[256,640]{1,0:T(8,128)(2,1)S(1)}, bf16[256,640]{1,0:T(8,128)(2,1)S(1)}, u32[]{:S(2)}, u32[]{:S(2)}) collective-permute-start(bf16[256,640]{1,0:T(8,128)(2,1)S(1)} %get-tuple-element.210), channel_id=1, source_target_pairs={{4,0},{8,4},{12,8},{5,1},{9,5},{13,9},{6,2},{10,6},{14,10},{7,3},{... | collective-permute-start | bytes 983048 | tf_op jit(solution)/shard_map/ppermute | solution.py:250
  199.4 15.8 %collective-permute-start.26 = (bf16[256,640]{1,0:T(8,128)(2,1)S(1)}, bf16[256,640]{1,0:T(8,128)(2,1)S(1)}, u32[]{:S(2)}, u32[]{:S(2)}) collective-permute-start(bf16[256,640]{1,0:T(8,128)(2,1)S(1)} %get-tuple-element.210), channel_id=1, source_target_pairs={{0,4},{4,8},{8,12},{1,5},{5,9},{9,13},{2,6},{6,10},{10,14},{3,7},{... | collective-permute-start | bytes 983048 | tf_op jit(solution)/shard_map/ppermute | solution.py:250
  202.4 12.7 %collective-permute-start.25 = (bf16[256,640]{1,0:T(8,128)(2,1)S(1)}, bf16[256,640]{1,0:T(8,128)(2,1)S(1)}, u32[]{:S(2)}, u32[]{:S(2)}) collective-permute-start(bf16[256,640]{1,0:T(8,128)(2,1)S(1)} %get-tuple-element.210), channel_id=1, source_target_pairs={{0,8},{4,12},{1,9},{5,13},{2,10},{6,14},{3,11},{7,15},{16,24},{20,... | collective-permute-start | bytes 983048 | tf_op jit(solution)/shard_map/ppermute | solution.py:250
  207.3 17.8 %collective-permute-start.13 = (bf16[256,1280]{1,0:T(8,128)(2,1)S(1)}, bf16[256,1280]{1,0:T(8,128)(2,1)S(1)}, u32[]{:S(2)}, u32[]{:S(2)}) collective-permute-start(bf16[256,1280]{1,0:T(8,128)(2,1)S(1)} %fusion.122), channel_id=1, source_target_pairs={{16,0},{17,1},{18,2},{19,3},{20,4},{21,5},{22,6},{23,7},{24,8},{25... | collective-permute-start | bytes 1966088 | tf_op jit(solution)/shard_map/ppermute | solution.py:250
  229.8 18.6 %collective-permute-start.22 = (bf16[256,640]{1,0:T(8,128)(2,1)S(1)}, bf16[256,640]{1,0:T(8,128)(2,1)S(1)}, u32[]{:S(2)}, u32[]{:S(2)}) collective-permute-start(bf16[256,640]{1,0:T(8,128)(2,1)S(1)} %get-tuple-element.109), channel_id=1, source_target_pairs={{8,0},{12,4},{9,1},{13,5},{10,2},{14,6},{11,3},{15,7},{24,16},{28,... | collective-permute-start | bytes 983048 | tf_op jit(solution)/shard_map/ppermute | solution.py:250
  231.1 17.2 %collective-permute-start.21 = (bf16[256,640]{1,0:T(8,128)(2,1)S(1)}, bf16[256,640]{1,0:T(8,128)(2,1)S(1)}, u32[]{:S(2)}, u32[]{:S(2)}) collective-permute-start(bf16[256,640]{1,0:T(8,128)(2,1)S(1)} %get-tuple-element.109), channel_id=1, source_target_pairs={{4,0},{8,4},{12,8},{5,1},{9,5},{13,9},{6,2},{10,6},{14,10},{7,3},{... | collective-permute-start | bytes 983048 | tf_op jit(solution)/shard_map/ppermute | solution.py:250
  232.4 15.8 %collective-permute-start.20 = (bf16[256,640]{1,0:T(8,128)(2,1)S(1)}, bf16[256,640]{1,0:T(8,128)(2,1)S(1)}, u32[]{:S(2)}, u32[]{:S(2)}) collective-permute-start(bf16[256,640]{1,0:T(8,128)(2,1)S(1)} %get-tuple-element.109), channel_id=1, source_target_pairs={{0,4},{4,8},{8,12},{1,5},{5,9},{9,13},{2,6},{6,10},{10,14},{3,7},{... | collective-permute-start | bytes 983048 | tf_op jit(solution)/shard_map/ppermute | solution.py:250
  235.5 12.7 %collective-permute-start.19 = (bf16[256,640]{1,0:T(8,128)(2,1)S(1)}, bf16[256,640]{1,0:T(8,128)(2,1)S(1)}, u32[]{:S(2)}, u32[]{:S(2)}) collective-permute-start(bf16[256,640]{1,0:T(8,128)(2,1)S(1)} %get-tuple-element.109), channel_id=1, source_target_pairs={{0,8},{4,12},{1,9},{5,13},{2,10},{6,14},{3,11},{7,15},{16,24},{20,... | collective-permute-start | bytes 983048 | tf_op jit(solution)/shard_map/ppermute | solution.py:250
  241.1 15.5 %collective-permute-start.34 = (bf16[256,1280]{1,0:T(8,128)(2,1)S(1)}, bf16[256,1280]{1,0:T(8,128)(2,1)S(1)}, u32[]{:S(2)}, u32[]{:S(2)}) collective-permute-start(bf16[256,1280]{1,0:T(8,128)(2,1)S(1)} %fusion.19), channel_id=1, source_target_pairs={{0,16},{1,17},{2,18},{3,19},{4,20},{5,21},{6,22},{7,23},{8,24},{9,... | collective-permute-start | bytes 1966088 | tf_op jit(solution)/shard_map/ppermute | solution.py:250
  258.6 19.1 %collective-permute-start.23 = (bf16[256,1280]{1,0:T(8,128)(2,1)S(1)}, bf16[256,1280]{1,0:T(8,128)(2,1)S(1)}, u32[]{:S(2)}, u32[]{:S(2)}) collective-permute-start(bf16[256,1280]{1,0:T(8,128)(2,1)S(1)} %fusion.123), channel_id=1, source_target_pairs={{16,0},{17,1},{18,2},{19,3},{20,4},{21,5},{22,6},{23,7},{24,8},{25... | collective-permute-start | bytes 1966088 | tf_op jit(solution)/shard_map/ppermute | solution.py:250
  280.7 18.6 %collective-permute-start.32 = (bf16[256,640]{1,0:T(8,128)(2,1)S(1)}, bf16[256,640]{1,0:T(8,128)(2,1)S(1)}, u32[]{:S(2)}, u32[]{:S(2)}) collective-permute-start(bf16[256,640]{1,0:T(8,128)(2,1)S(1)} %get-tuple-element.111), channel_id=1, source_target_pairs={{8,0},{12,4},{9,1},{13,5},{10,2},{14,6},{11,3},{15,7},{24,16},{28,... | collective-permute-start | bytes 983048 | tf_op jit(solution)/shard_map/ppermute | solution.py:250
  282.0 17.2 %collective-permute-start.31 = (bf16[256,640]{1,0:T(8,128)(2,1)S(1)}, bf16[256,640]{1,0:T(8,128)(2,1)S(1)}, u32[]{:S(2)}, u32[]{:S(2)}) collective-permute-start(bf16[256,640]{1,0:T(8,128)(2,1)S(1)} %get-tuple-element.111), channel_id=1, source_target_pairs={{4,0},{8,4},{12,8},{5,1},{9,5},{13,9},{6,2},{10,6},{14,10},{7,3},{... | collective-permute-start | bytes 983048 | tf_op jit(solution)/shard_map/ppermute | solution.py:250
  283.3 15.8 %collective-permute-start.30 = (bf16[256,640]{1,0:T(8,128)(2,1)S(1)}, bf16[256,640]{1,0:T(8,128)(2,1)S(1)}, u32[]{:S(2)}, u32[]{:S(2)}) collective-permute-start(bf16[256,640]{1,0:T(8,128)(2,1)S(1)} %get-tuple-element.111), channel_id=1, source_target_pairs={{0,4},{4,8},{8,12},{1,5},{5,9},{9,13},{2,6},{6,10},{10,14},{3,7},{... | collective-permute-start | bytes 983048 | tf_op jit(solution)/shard_map/ppermute | solution.py:250
  286.3 12.7 %collective-permute-start.29 = (bf16[256,640]{1,0:T(8,128)(2,1)S(1)}, bf16[256,640]{1,0:T(8,128)(2,1)S(1)}, u32[]{:S(2)}, u32[]{:S(2)}) collective-permute-start(bf16[256,640]{1,0:T(8,128)(2,1)S(1)} %get-tuple-element.111), channel_id=1, source_target_pairs={{0,8},{4,12},{1,9},{5,13},{2,10},{6,14},{3,11},{7,15},{16,24},{20,... | collective-permute-start | bytes 983048 | tf_op jit(solution)/shard_map/ppermute | solution.py:250
  315.6 18.6 %collective-permute-start.38 = (bf16[256,640]{1,0:T(8,128)(2,1)S(1)}, bf16[256,640]{1,0:T(8,128)(2,1)S(1)}, u32[]{:S(2)}, u32[]{:S(2)}) collective-permute-start(bf16[256,640]{1,0:T(8,128)(2,1)S(1)} %get-tuple-element.207), channel_id=1, source_target_pairs={{8,0},{12,4},{9,1},{13,5},{10,2},{14,6},{11,3},{15,7},{24,16},{28,... | collective-permute-start | bytes 983048 | tf_op jit(solution)/shard_map/ppermute | solution.py:250
  316.9 17.3 %collective-permute-start.37 = (bf16[256,640]{1,0:T(8,128)(2,1)S(1)}, bf16[256,640]{1,0:T(8,128)(2,1)S(1)}, u32[]{:S(2)}, u32[]{:S(2)}) collective-permute-start(bf16[256,640]{1,0:T(8,128)(2,1)S(1)} %get-tuple-element.207), channel_id=1, source_target_pairs={{4,0},{8,4},{12,8},{5,1},{9,5},{13,9},{6,2},{10,6},{14,10},{7,3},{... | collective-permute-start | bytes 983048 | tf_op jit(solution)/shard_map/ppermute | solution.py:250
  318.2 15.8 %collective-permute-start.36 = (bf16[256,640]{1,0:T(8,128)(2,1)S(1)}, bf16[256,640]{1,0:T(8,128)(2,1)S(1)}, u32[]{:S(2)}, u32[]{:S(2)}) collective-permute-start(bf16[256,640]{1,0:T(8,128)(2,1)S(1)} %get-tuple-element.207), channel_id=1, source_target_pairs={{0,4},{4,8},{8,12},{1,5},{5,9},{9,13},{2,6},{6,10},{10,14},{3,7},{... | collective-permute-start | bytes 983048 | tf_op jit(solution)/shard_map/ppermute | solution.py:250
  321.3 12.7 %collective-permute-start.35 = (bf16[256,640]{1,0:T(8,128)(2,1)S(1)}, bf16[256,640]{1,0:T(8,128)(2,1)S(1)}, u32[]{:S(2)}, u32[]{:S(2)}) collective-permute-start(bf16[256,640]{1,0:T(8,128)(2,1)S(1)} %get-tuple-element.207), channel_id=1, source_target_pairs={{0,8},{4,12},{1,9},{5,13},{2,10},{6,14},{3,11},{7,15},{16,24},{20,... | collective-permute-start | bytes 983048 | tf_op jit(solution)/shard_map/ppermute | solution.py:250
  327.2 17.6 %collective-permute-start.33 = (bf16[256,1280]{1,0:T(8,128)(2,1)S(1)}, bf16[256,1280]{1,0:T(8,128)(2,1)S(1)}, u32[]{:S(2)}, u32[]{:S(2)}) collective-permute-start(bf16[256,1280]{1,0:T(8,128)(2,1)S(1)} %fusion.124), channel_id=1, source_target_pairs={{16,0},{17,1},{18,2},{19,3},{20,4},{21,5},{22,6},{23,7},{24,8},{25... | collective-permute-start | bytes 1966088 | tf_op jit(solution)/shard_map/ppermute | solution.py:250
  335.5 38.4 %copy-start.3 = (bf16[256,3200]{1,0:T(8,128)(2,1)}, bf16[256,3200]{1,0:T(8,128)(2,1)S(1)}, u32[]{:S(2)}) copy-start(bf16[256,3200]{1,0:T(8,128)(2,1)S(1)} %multiply_dynamic-update-slice_fusion.10) | copy-start | bytes 4915204
  347.8 9.7 %collective-permute-start.39 = (bf16[256,640]{1,0:T(8,128)(2,1)S(1)}, bf16[256,640]{1,0:T(8,128)(2,1)S(1)}, u32[]{:S(2)}, u32[]{:S(2)}) collective-permute-start(bf16[256,640]{1,0:T(8,128)(2,1)S(1)} %get-tuple-element.113), channel_id=1, source_target_pairs={{0,8},{4,12},{1,9},{5,13},{2,10},{6,14},{3,11},{7,15},{16,24},{20,... | collective-permute-start | bytes 983048 | tf_op jit(solution)/shard_map/ppermute | solution.py:250
  349.6 8.0 %collective-permute-start.40 = (bf16[256,640]{1,0:T(8,128)(2,1)S(1)}, bf16[256,640]{1,0:T(8,128)(2,1)S(1)}, u32[]{:S(2)}, u32[]{:S(2)}) collective-permute-start(bf16[256,640]{1,0:T(8,128)(2,1)S(1)} %get-tuple-element.113), channel_id=1, source_target_pairs={{0,4},{4,8},{8,12},{1,5},{5,9},{9,13},{2,6},{6,10},{10,14},{3,7},{... | collective-permute-start | bytes 983048 | tf_op jit(solution)/shard_map/ppermute | solution.py:250
  351.0 11.6 %collective-permute-start.42 = (bf16[256,640]{1,0:T(8,128)(2,1)S(1)}, bf16[256,640]{1,0:T(8,128)(2,1)S(1)}, u32[]{:S(2)}, u32[]{:S(2)}) collective-permute-start(bf16[256,640]{1,0:T(8,128)(2,1)S(1)} %get-tuple-element.113), channel_id=1, source_target_pairs={{8,0},{12,4},{9,1},{13,5},{10,2},{14,6},{11,3},{15,7},{24,16},{28,... | collective-permute-start | bytes 983048 | tf_op jit(solution)/shard_map/ppermute | solution.py:250
  352.3 5.5 collective-permute-start.41
  372.3 16.9 %collective-permute-start.43 = (bf16[256,1280]{1,0:T(8,128)(2,1)S(1)}, bf16[256,1280]{1,0:T(8,128)(2,1)S(1)}, u32[]{:S(2)}, u32[]{:S(2)}) collective-permute-start(bf16[256,1280]{1,0:T(8,128)(2,1)S(1)} %fusion.125), channel_id=1, source_target_pairs={{16,0},{17,1},{18,2},{19,3},{20,4},{21,5},{22,6},{23,7},{24,8},{25... | collective-permute-start | bytes 1966088 | tf_op jit(solution)/shard_map/ppermute | solution.py:250
  379.4 10.1 %copy-start.70 = (f32[256]{0:T(256)S(1)}, f32[256]{0:T(256)}, u32[]{:S(2)}) copy-start(f32[256]{0:T(256)} %get-tuple-element.232) | copy-start | bytes 3076
  389.4 14.4 %copy-start.7 = (bf16[256,1280]{1,0:T(8,128)(2,1)}, bf16[256,1280]{1,0:T(8,128)(2,1)S(1)}, u32[]{:S(2)}) copy-start(bf16[256,1280]{1,0:T(8,128)(2,1)S(1)} %get-tuple-element.133) | copy-start | bytes 1966084
  392.3 12.2 %copy-start.28 = (f32[1280]{0:T(1024)S(1)}, f32[1280]{0:T(1024)}, u32[]{:S(2)}) copy-start(f32[1280]{0:T(1024)} %get-tuple-element.29) | copy-start | bytes 15364
  392.3 12.2 %copy-start.2 = (f32[640,1280]{1,0:T(8,128)S(1)}, f32[640,1280]{1,0:T(8,128)}, u32[]{:S(2)}) copy-start(f32[640,1280]{1,0:T(8,128)} %convolution_select_fusion.4) | copy-start | bytes 9830404
  392.3 12.2 %copy-start.12 = (bf16[256,640]{1,0:T(8,128)(2,1)S(1)}, bf16[256,640]{1,0:T(8,128)(2,1)}, u32[]{:S(2)}) copy-start(bf16[256,640]{1,0:T(8,128)(2,1)} %copy-done.11) | copy-start | bytes 983044
  392.3 19.9 %collective-permute-start.47 = (bf16[256,640]{1,0:T(8,128)(2,1)S(1)}, bf16[256,640]{1,0:T(8,128)(2,1)S(1)}, u32[]{:S(2)}, u32[]{:S(2)}) collective-permute-start(bf16[256,640]{1,0:T(8,128)(2,1)S(1)} %get-tuple-element.115), channel_id=1, source_target_pairs={{8,0},{12,4},{9,1},{13,5},{10,2},{14,6},{11,3},{15,7},{24,16},{28,... | collective-permute-start | bytes 983048 | tf_op jit(solution)/shard_map/ppermute | solution.py:250
  393.9 18.3 %collective-permute-start.46 = (bf16[256,640]{1,0:T(8,128)(2,1)S(1)}, bf16[256,640]{1,0:T(8,128)(2,1)S(1)}, u32[]{:S(2)}, u32[]{:S(2)}) collective-permute-start(bf16[256,640]{1,0:T(8,128)(2,1)S(1)} %get-tuple-element.115), channel_id=1, source_target_pairs={{4,0},{8,4},{12,8},{5,1},{9,5},{13,9},{6,2},{10,6},{14,10},{7,3},{... | collective-permute-start | bytes 983048 | tf_op jit(solution)/shard_map/ppermute | solution.py:250
  395.2 16.8 %collective-permute-start.45 = (bf16[256,640]{1,0:T(8,128)(2,1)S(1)}, bf16[256,640]{1,0:T(8,128)(2,1)S(1)}, u32[]{:S(2)}, u32[]{:S(2)}) collective-permute-start(bf16[256,640]{1,0:T(8,128)(2,1)S(1)} %get-tuple-element.115), channel_id=1, source_target_pairs={{0,4},{4,8},{8,12},{1,5},{5,9},{9,13},{2,6},{6,10},{10,14},{3,7},{... | collective-permute-start | bytes 983048 | tf_op jit(solution)/shard_map/ppermute | solution.py:250
  400.1 11.8 %collective-permute-start.44 = (bf16[256,640]{1,0:T(8,128)(2,1)S(1)}, bf16[256,640]{1,0:T(8,128)(2,1)S(1)}, u32[]{:S(2)}, u32[]{:S(2)}) collective-permute-start(bf16[256,640]{1,0:T(8,128)(2,1)S(1)} %get-tuple-element.115), channel_id=1, source_target_pairs={{0,8},{4,12},{1,9},{5,13},{2,10},{6,14},{3,11},{7,15},{16,24},{20,... | collective-permute-start | bytes 983048 | tf_op jit(solution)/shard_map/ppermute | solution.py:250
  540.7 9.6 %slice-start = ((s8[7536640]{0:T(1024)(128)(4,1)}), s8[4194304]{0:T(1024)(128)(4,1)S(1)}, s32[]{:S(2)}) async-start(s8[7536640]{0:T(1024)(128)(4,1)} %bitcast.347), calls=%async_computation | async-start | bytes 8388608
  (60 other events, 167.8 us)

commit v2 on v1

v2 whole, which is shorter than its diff:
```python
import functools

import jax
import jax.numpy as jnp
from jax import lax
from jax.experimental import pallas as pl
from jax.experimental.pallas import tpu as pltpu
from jax.sharding import PartitionSpec as P

KERNEL = 5
VOCAB = 30
DILATION_STEP = 128
ITEMS = 4
EPSILON = 1e-05
ROOT_HALF = 0.7071067811865476
HALF_LOG = -0.7213475204444817
ROOT_TAU = 0.3989422804014327

MESH = pl.DeviceIdType.MESH
WIDE = 640
SUBS = 2
VMEM_BYTES = 64 << 20


def far_rows(left, own, right, offset):
    edge, positions = left.shape[0], own.shape[0]
    first, last = offset + edge, offset + edge + positions
    pieces, at = [], 0
    for block in (left, own, right):
        lo, hi = max(first, at), min(last, at + block.shape[0])
        if lo < hi:
            pieces.append(block[lo - at : hi - at])
        at += block.shape[0]
    return pieces[0] if len(pieces) == 1 else jnp.concatenate(pieces, axis=0)


def act_forward(values, gain, shift, real):
    scale = 1.0 / values.shape[1]
    centred = values - jnp.sum(values, axis=1, keepdims=True) * scale
    spread = jnp.sum(centred * centred, axis=1, keepdims=True) * scale
    inverse = lax.rsqrt(spread + EPSILON)
    hat = centred * inverse
    moved = hat * gain + shift
    below = (0.5 + 0.5 * lax.erf(moved * ROOT_HALF)) * real
    density = jnp.exp2(moved * moved * HALF_LOG) * (ROOT_TAU * real)
    return moved * below, hat, below + moved * density, inverse


def fold(values):
    rows, columns = values.shape
    return jnp.sum(values.reshape(rows // 8, 8, columns), axis=0)


def act_backward(grad, hat, slope, inverse, gain, gain_sum, shift_sum):
    scale = 1.0 / grad.shape[1]
    hat = hat.astype(jnp.float32)
    moved = grad * slope.astype(jnp.float32)
    turned = moved * hat
    shift_sum[...] += fold(moved)
    gain_sum[...] += fold(turned)
    mean = jnp.sum(moved * gain, axis=1, keepdims=True) * scale
    tilt = jnp.sum(turned * gain, axis=1, keepdims=True) * scale
    return inverse * (moved * gain - mean - hat * tilt)


def dot_nn(a, b):
    return jnp.dot(a, b, preferred_element_type=jnp.float32)


def dot_nt(a, b):
    return lax.dot_general(a, b, (((1,), (1,)), ((), ())), preferred_element_type=jnp.float32)


def dot_tn(a, b):
    return lax.dot_general(a, b, (((0,), (0,)), ((), ())), preferred_element_type=jnp.float32)


def blocks_kernel(
    edge,
    boundary, lengths, masked, residues, readout,
    first_gain, first_shift, in_weight, in_bias, second_gain, second_shift, conv_weight, conv_bias,
    third_gain, third_shift, out_weight, out_bias,
    result, big, small,
    buf, w_in, w_conv, w_out, total, hat1, slope1, act1, taps, back_taps,
    hat2, slope2, hat3, slope3, act3, grad1, grad2, rim_left, rim_right, near, masks, spreads,
    sums_wide, sums, hits, tally, stage,
    load_sem, weight_sem, result_sem, hand_send, hand_recv, rim_send, rim_recv, stage_sem,
):
    section = lax.axis_index("section")
    seq = lax.axis_index("seq")
    dp = lax.axis_index("dp")
    n_seq = lax.axis_size("seq")
    rows, positions = buf.shape[0] // 2, buf.shape[1]
    hidden = w_in.shape[1]
    leading = section == 0
    trailing = section == 1
    row_len = n_seq * positions
    first_position = seq * positions
    reach = edge // positions
    dilation = jnp.where(leading, 1, DILATION_STEP)

    def load(m):
        return pltpu.make_async_copy(boundary.at[0, m], buf.at[section * rows + m], load_sem.at[m])

    weight_loads = [
        pltpu.make_async_copy(source.at[0], target, weight_sem.at[i])
        for i, (source, target) in enumerate(((in_weight, w_in), (conv_weight, w_conv), (out_weight, w_out)))
    ]
    load(0).start()
    for copy in weight_loads:
        copy.start()
    for m in range(1, rows):
        load(m).start()

    def partner():
        return (1 - section, seq, dp)

    barrier = pltpu.get_barrier_semaphore()
    pl.semaphore_signal(barrier, inc=1, device_id=partner(), device_id_type=MESH)
    greeted = 1
    for j in range(1, reach + 1):
        for side in (-j, j):
            on = (seq + side >= 0) & (seq + side < n_seq)
            greeted = greeted + on.astype(jnp.int32)

            @pl.when(on)
            def _():
                pl.semaphore_signal(barrier, inc=1, device_id=(section, seq + side, dp), device_id_type=MESH)

    sums_wide[...] = jnp.zeros_like(sums_wide)
    sums[...] = jnp.zeros_like(sums)
    hits[...] = jnp.zeros_like(hits)
    tally[...] = jnp.zeros_like(tally)

    @pl.when(seq < reach)
    def _():
        rim_left[...] = jnp.zeros_like(rim_left)

    @pl.when(seq >= n_seq - reach)
    def _():
        rim_right[...] = jnp.zeros_like(rim_right)

    lane = lax.broadcasted_iota(jnp.int32, (positions, 128), 1)
    place = lax.broadcasted_iota(jnp.int32, (positions, 128), 0) + first_position
    other = place + (lane - KERNEL // 2) * dilation
    for m in range(rows):
        end = 0
        here = jnp.zeros((positions, 128), jnp.int32)
        there = jnp.zeros((positions, 128), jnp.int32)
        for j in range(ITEMS):
            end = end + lengths[m, j]
            here = here + (place >= end).astype(jnp.int32)
            there = there + (other >= end).astype(jnp.int32)
        counts = (here == there) & (here < ITEMS) & (other >= 0) & (other < row_len)
        masks[m] = counts.astype(jnp.float32)

    pl.semaphore_wait(barrier, greeted)

    def hand(m):
        forward = pltpu.make_async_remote_copy(
            src_ref=buf.at[m], dst_ref=buf.at[m], send_sem=hand_send.at[m], recv_sem=hand_recv.at[m],
            device_id=partner(), device_id_type=MESH)
        backward = pltpu.make_async_remote_copy(
            src_ref=hat1.at[m], dst_ref=buf.at[rows + m], send_sem=hand_send.at[m], recv_sem=hand_recv.at[m],
            device_id=partner(), device_id_type=MESH)
        return forward, backward

    def rim_copies(backward, m):
        slot = 2 * backward + m % 2
        own = grad2.at[m] if backward else taps.at[m, KERNEL // 2]
        turn = backward * rows + m

        def copy(source, target, index, to):
            return pltpu.make_async_remote_copy(
                src_ref=source, dst_ref=target, send_sem=rim_send.at[turn, index], recv_sem=rim_recv.at[turn, index],
                device_id=(section, to, dp), device_id_type=MESH)

        near_copies = [
            (seq + 1 < n_seq, seq >= 1,
             copy(own.at[pl.ds(positions - 16, 16)], rim_left.at[slot, pl.ds(edge - 16, 16)], 0, seq + 1)),
            (seq >= 1, seq + 1 < n_seq,
             copy(own.at[pl.ds(0, 16)], rim_right.at[slot, pl.ds(0, 16)], 1, seq - 1)),
        ]
        far_copies = []
        for j in range(1, reach + 1):
            far_copies.append((
                seq + j < n_seq, seq >= j,
                copy(own, rim_left.at[slot, pl.ds(edge - j * positions, positions)], 2 * j - 2, seq + j)))
            far_copies.append((
                seq >= j, seq + j < n_seq,
                copy(own, rim_right.at[slot, pl.ds((j - 1) * positions, positions)], 2 * j - 1, seq - j)))
        return near_copies, far_copies

    def rim_start(backward, m):
        for here, copies in zip((leading, trailing), rim_copies(backward, m)):
            for sends, _, copy in copies:
                pl.when(here & sends)(copy.start)

    def rim_wait(backward, m):
        for here, copies in zip((leading, trailing), rim_copies(backward, m)):
            for sends, receives, copy in copies:
                pl.when(here & receives)(copy.wait_recv)
                pl.when(here & sends)(copy.wait_send)

    def gather(backward, m, own, store):
        slot = 2 * backward + m % 2
        mask = masks[m]

        @pl.when(leading)
        def _():
            near[16 : 16 + positions] = own().astype(jnp.float32)
            near[0:16] = rim_left[slot, edge - 16 : edge].astype(jnp.float32)
            near[16 + positions : 32 + positions] = rim_right[slot, 0:16].astype(jnp.float32)
            for k in range(KERNEL):
                if k != KERNEL // 2:
                    at = 16 + k - KERNEL // 2
                    store(k, jnp.where(mask[:, k : k + 1] > 0, near[at : at + positions], 0.0))

        @pl.when(trailing)
        def _():
            for k in range(KERNEL):
                if k != KERNEL // 2:
                    piece = far_rows(rim_left[slot], own(), rim_right[slot], (k - KERNEL // 2) * DILATION_STEP)
                    store(k, jnp.where(mask[:, k : k + 1] > 0, piece.astype(jnp.float32), 0.0))

    def real_of(m):
        return masks[m][:, KERNEL // 2 : KERNEL // 2 + 1]

    def forward_start(m):
        @pl.when(leading)
        def _():
            load(m).wait()

        @pl.when(trailing)
        def _():
            hand(m)[0].wait_recv()

        real = real_of(m)
        act, hat, slope, inverse = act_forward(buf[m].astype(jnp.float32), first_gain[...], first_shift[...], real)
        act1[m] = act.astype(jnp.bfloat16)
        hat1[m] = hat.astype(jnp.bfloat16)
        slope1[m] = slope.astype(jnp.bfloat16)
        spreads[m, 0] = inverse
        pre = dot_nn(act1[m], w_in[...]) + in_bias[...]
        act, hat, slope, inverse = act_forward(pre, second_gain[...], second_shift[...], real)
        taps[m, KERNEL // 2] = act.astype(jnp.bfloat16)
        rim_start(0, m)
        hat2[m] = hat.astype(jnp.bfloat16)
        slope2[m] = slope.astype(jnp.bfloat16)
        spreads[m, 1] = inverse

    def forward_end(m):
        def store(k, value):
            taps[m, k] = value.astype(jnp.bfloat16)

        rim_wait(0, m)
        gather(0, m, lambda: taps[m, KERNEL // 2], store)
        pre = conv_bias[...]
        for k in range(KERNEL):
            pre = pre + dot_nn(taps[m, k], w_conv[k])
        act, hat, slope, inverse = act_forward(pre, third_gain[...], third_shift[...], real_of(m))
        act3[m] = act.astype(jnp.bfloat16)
        hat3[m] = hat.astype(jnp.bfloat16)
        slope3[m] = slope.astype(jnp.bfloat16)
        spreads[m, 2] = inverse
        out = buf[m].astype(jnp.float32) + (dot_nn(act3[m], w_out[...]) + out_bias[...])
        buf[m] = out.astype(jnp.bfloat16)

        @pl.when(leading)
        def _():
            hand(m)[0].start()

        @pl.when(trailing)
        def _():
            pltpu.make_async_copy(buf.at[m], result.at[0, m], result_sem.at[m]).start()
            logits = dot_nt(readout[...], buf[m])
            kind = lax.broadcasted_iota(jnp.int32, logits.shape, 0)
            logits = jnp.where(kind < VOCAB, logits, -1e30)
            odds = jnp.exp(logits - jnp.max(logits, axis=0, keepdims=True))
            odds = odds / jnp.sum(odds, axis=0, keepdims=True)
            end = lengths[m, 0]
            for j in range(1, ITEMS):
                end = end + lengths[m, j]
            spot = lax.broadcasted_iota(jnp.int32, (1, positions), 1) + first_position
            chosen = jnp.where(spot < end, masked[pl.ds(m, 1)].astype(jnp.float32), 0.0)
            chosen = jnp.where(kind == residues[pl.ds(m, 1)], chosen, 0.0)
            hits[...] += chosen * odds
            tally[...] += chosen

    def backward_start(m):
        @pl.when(leading)
        def _():
            hand(m)[1].wait_recv()

        @pl.when(trailing)
        def _():
            load(m).wait()

        sums_wide[2] += fold(buf[rows + m].astype(jnp.float32))
        grad = dot_nt(buf[rows + m], w_out[...])
        low = act_backward(
            grad, hat3[m], slope3[m], spreads[m, 2], third_gain[...], sums.at[4], sums.at[5]
        ).astype(jnp.bfloat16)
        grad2[m] = low
        back_taps[KERNEL // 2] = low
        rim_start(1, m)
        sums[3] += fold(low.astype(jnp.float32))

    def backward_end(m):
        def store(k, value):
            back_taps[k] = value.astype(jnp.bfloat16)

        rim_wait(1, m)
        gather(1, m, lambda: grad2[m], store)
        grad = dot_nt(back_taps[0], w_conv[KERNEL - 1])
        for k in range(1, KERNEL):
            grad = grad + dot_nt(back_taps[k], w_conv[KERNEL - 1 - k])
        low = act_backward(
            grad, hat2[m], slope2[m], spreads[m, 1], second_gain[...], sums.at[1], sums.at[2]
        ).astype(jnp.bfloat16)
        grad1[m] = low
        grad = dot_nt(low, w_in[...])
        grad = act_backward(
            grad, hat1[m], slope1[m], spreads[m, 0], first_gain[...], sums_wide.at[0], sums_wide.at[1]
        )
        hat1[m] = (buf[rows + m].astype(jnp.float32) + grad).astype(jnp.bfloat16)

        @pl.when(leading)
        def _():
            pltpu.make_async_copy(hat1.at[m], result.at[0, m], result_sem.at[m]).start()

        @pl.when(trailing)
        def _():
            hand(m)[1].start()

        sums[0] += fold(low.astype(jnp.float32))

    wide = buf.shape[2] // hidden

    def add_block(block, value):
        total[pl.ds(block * hidden, hidden)] += value

    def weights_out(m):
        for j in range(wide):
            add_block(wide + KERNEL + j, dot_tn(act3[m], buf[rows + m, :, j * hidden : (j + 1) * hidden]))

    def weights_rest(m):
        for k in range(KERNEL):
            add_block(wide + k, dot_tn(taps[m, k], grad2[m]))
        for j in range(wide):
            add_block(j, dot_tn(act1[m, :, j * hidden : (j + 1) * hidden], grad1[m]))

    def step(i, carry):
        m_front = i - 1
        m_back = jnp.where(leading, i - 1 - rows, i - 1)
        m_next = i
        m_sum = i - 1 - rows

        def on(m, allowed=True):
            return (m >= 0) & (m < rows) & allowed

        @pl.when(i == 1)
        def _():
            weight_loads[1].wait()
            weight_loads[2].wait()

        @pl.when(on(m_front))
        def _():
            forward_end(m_front)

        @pl.when(on(m_back))
        def _():
            backward_start(m_back)

        @pl.when(i == 0)
        def _():
            weight_loads[0].wait()

        @pl.when(on(m_next))
        def _():
            forward_start(m_next)

        @pl.when((leading & (i == 3)) | (trailing & (i == 0)))
        def _():
            total[...] = jnp.zeros_like(total)

        @pl.when(on(m_sum))
        def _():
            weights_out(m_sum)

        @pl.when(on(m_back))
        def _():
            backward_end(m_back)

        @pl.when(on(m_sum))
        def _():
            weights_rest(m_sum)

        return carry

    lax.fori_loop(0, 2 * rows + 1, step, 0)

    blocks = wide + KERNEL + wide

    def give(b, slot):
        return pltpu.make_async_copy(stage.at[slot], big.at[pl.ds(b * hidden, hidden)], stage_sem.at[slot])

    for b in range(blocks):
        slot = b % 2
        if b >= 2:
            give(b - 2, slot).wait()
        stage[slot] = total[b * hidden : (b + 1) * hidden].astype(jnp.bfloat16)
        give(b, slot).start()
    for b in range(blocks - 2, blocks):
        give(b, b % 2).wait()
    spare = big.shape[0] - blocks * hidden
    stage[0, :spare] = jnp.zeros((spare, hidden), jnp.bfloat16)
    tail = pltpu.make_async_copy(stage.at[0, pl.ds(0, spare)], big.at[pl.ds(blocks * hidden, spare)], stage_sem.at[0])
    tail.start()
    for i in range(3):
        small[i : i + 1, :] = jnp.sum(sums_wide[i], axis=0, keepdims=True)
    for i in range(6):
        small[3 + i // 2 : 4 + i // 2, (i % 2) * hidden : (i % 2 + 1) * hidden] = jnp.sum(sums[i], axis=0, keepdims=True)
    small[6:8, :] = jnp.zeros((2, small.shape[1]), jnp.float32)
    ones = jnp.ones((8, positions), jnp.float32)
    for i, counted in ((6, hits), (7, tally)):
        row = lax.dot_general(
            ones, counted[...], (((1,), (1,)), ((), ())), precision=lax.Precision.HIGHEST,
            preferred_element_type=jnp.float32)
        small[i : i + 1, 0 : counted.shape[0]] = row[0:1]
    tail.wait()
    for m in range(rows):
        @pl.when(leading)
        def _():
            hand(m)[0].wait_send()
            pltpu.make_async_copy(hat1.at[m], result.at[0, m], result_sem.at[m]).wait()

        @pl.when(trailing)
        def _():
            hand(m)[1].wait_send()
            pltpu.make_async_copy(buf.at[m], result.at[0, m], result_sem.at[m]).wait()


def run_blocks(args, big_rows, cid=0):
    boundary, in_weight, conv_weight = args[0], args[7], args[11]
    _, rows, positions, width = boundary.shape
    hidden = in_weight.shape[2]
    edge = KERNEL // 2 * DILATION_STEP
    assert edge % positions == 0 and positions % 16 == 0 and width % hidden == 0
    reach = edge // positions
    low, full = jnp.bfloat16, jnp.float32
    wide_rows = pltpu.VMEM((rows, positions, width), low)
    thin_rows = pltpu.VMEM((rows, positions, hidden), low)
    blocks = (2 * width // hidden + KERNEL) * hidden
    where = [pl.ANY, pltpu.SMEM] + [pltpu.VMEM] * 15
    for i in (7, 11, 15):
        where[i] = pl.ANY
    return pl.pallas_call(
        functools.partial(blocks_kernel, edge),
        out_shape=(
            jax.ShapeDtypeStruct(boundary.shape, low),
            jax.ShapeDtypeStruct((big_rows, hidden), low),
            jax.ShapeDtypeStruct((8, width), full),
        ),
        in_specs=[pl.BlockSpec(memory_space=space) for space in where],
        out_specs=[pl.BlockSpec(memory_space=space) for space in (pl.ANY, pl.ANY, pltpu.VMEM)],
        scratch_shapes=[
            pltpu.VMEM((2 * rows, positions, width), low),
            pltpu.VMEM((width, hidden), low),
            pltpu.VMEM((KERNEL, hidden, hidden), low),
            pltpu.VMEM((hidden, width), low),
            pltpu.VMEM((blocks, hidden), full),
            wide_rows, wide_rows, wide_rows,
            pltpu.VMEM((rows, KERNEL, positions, hidden), low),
            pltpu.VMEM((KERNEL, positions, hidden), low),
            thin_rows, thin_rows, thin_rows, thin_rows, thin_rows, thin_rows, thin_rows,
            pltpu.VMEM((4, edge, hidden), low),
            pltpu.VMEM((4, edge, hidden), low),
            pltpu.VMEM((positions + 32, hidden), full),
            pltpu.VMEM((rows, positions, 128), full),
            pltpu.VMEM((rows, 3, positions, 1), full),
            pltpu.VMEM((3, 8, width), full),
            pltpu.VMEM((6, 8, hidden), full),
            pltpu.VMEM((32, positions), full),
            pltpu.VMEM((32, positions), full),
            pltpu.VMEM((2, hidden, hidden), low),
            pltpu.SemaphoreType.DMA((rows,)),
            pltpu.SemaphoreType.DMA((3,)),
            pltpu.SemaphoreType.DMA((rows,)),
            pltpu.SemaphoreType.DMA((rows,)),
            pltpu.SemaphoreType.DMA((rows,)),
            pltpu.SemaphoreType.DMA((2 * rows, 2 * reach)),
            pltpu.SemaphoreType.DMA((2 * rows, 2 * reach)),
            pltpu.SemaphoreType.DMA((2,)),
        ],
        compiler_params=pltpu.CompilerParams(
            collective_id=cid, has_side_effects=True, vmem_limit_bytes=VMEM_BYTES),
    )(*args)


def ring_sizes(rows, nodes):
    units = -(-rows // (nodes * 16))
    long = -(-units // 2)
    return [[16 * ((way + i) // SUBS) for i in range(SUBS)] for way in (long, units - long)]


def ring_kernel(ny, nz, sizes, w_ref, s_ref, o_ref, t_ref, core_land, *rest):
    nodes = ny * nz
    flows = [(way, i) for way in range(2) for i in range(len(sizes[way])) if sizes[way][i]]
    lands = rest[:len(flows)]
    small_land, core_send, core_recv, ring_send, ring_recv, back_send, back_recv, small_send, small_recv = rest[len(flows):]
    s = lax.axis_index("section")
    q = lax.axis_index("seq")
    d = lax.axis_index("dp")
    core = q % 2
    ypos = q // 2
    odd = ypos % 2
    spot = ypos * nz + d + odd * (nz - 1 - 2 * d)

    def at_spot(place):
        yy = place // nz
        dd = place % nz
        dd = dd + (yy % 2) * (nz - 1 - 2 * dd)
        return (s, yy * 2 + core, dd)

    other_core = (s, q + 1 - 2 * core, d)
    other_x = (1 - s, q, d)
    ahead = at_spot((spot + 1) % nodes)
    behind = at_spot((spot + nodes - 1) % nodes)
    half = sum(sum(way) for way in sizes) * nodes
    turn = [1 - 2 * core, 2 * core - 1]

    peers = [other_core]
    reach = 1
    while reach < ny:
        peers.append((s, q + 2 * reach - 4 * reach * ((ypos // reach) % 2), d))
        reach *= 2
    reach = 1
    while reach < nz:
        peers.append((s, q, d + reach - 2 * reach * ((d // reach) % 2)))
        reach *= 2

    barrier = pltpu.get_barrier_semaphore()
    greet = [other_core, other_x, ahead, behind] + peers[1:]
    for peer in greet:
        pl.semaphore_signal(barrier, inc=1, device_id=peer, device_id_type=MESH)
    pl.semaphore_wait(barrier, len(greet))

    first = {}
    at = 0
    for way, i in flows:
        first[way, i] = at
        at += sizes[way][i] * nodes

    def rows_of(flow, side, shard):
        way, i = flow
        return pl.ds(pl.multiple_of(side * half + first[flow] + shard * sizes[way][i], 16), sizes[way][i])

    def shard_at(flow, step):
        return (spot + 2 * nodes - turn[flow[0]] * step) % nodes

    def next_of(flow):
        return at_spot((spot + nodes + turn[flow[0]]) % nodes)

    def core_copy(f, shard):
        flow = flows[f]
        return pltpu.make_async_remote_copy(
            src_ref=w_ref.at[rows_of(flow, 1 - core, shard)],
            dst_ref=core_land.at[rows_of(flow, 0, shard)],
            send_sem=core_send.at[f, shard], recv_sem=core_recv.at[f, shard],
            device_id=other_core, device_id_type=MESH)

    def ring_copy(f, step, shard):
        flow = flows[f]
        return pltpu.make_async_remote_copy(
            src_ref=w_ref.at[rows_of(flow, core, shard)],
            dst_ref=lands[f].at[step],
            send_sem=ring_send.at[f, step], recv_sem=ring_recv.at[f, step],
            device_id=next_of(flow), device_id_type=MESH)

    def back_copy(f, step, shard):
        block = o_ref.at[rows_of(flows[f], core, shard)]
        return pltpu.make_async_remote_copy(
            src_ref=block, dst_ref=block,
            send_sem=ring_send.at[f, nodes - 1 + step], recv_sem=ring_recv.at[f, nodes - 1 + step],
            device_id=next_of(flows[f]), device_id_type=MESH)

    def over_copy(f, shard):
        block = o_ref.at[rows_of(flows[f], core, shard)]
        return pltpu.make_async_remote_copy(
            src_ref=block, dst_ref=block,
            send_sem=back_send.at[f, shard], recv_sem=back_recv.at[f, shard],
            device_id=other_core, device_id_type=MESH)

    def add(f, shard, step, target):
        flow = flows[f]
        rows = sizes[flow[0]][flow[1]]
        here = rows_of(flow, core, shard).start
        there = rows_of(flow, 0, shard).start

        def body(i, carry):
            off = pl.multiple_of(i * 16, 16)
            total = w_ref[pl.ds(here + off, 16)].astype(jnp.float32)
            total = total + core_land[pl.ds(there + off, 16)].astype(jnp.float32)
            if step is not None:
                total = total + lands[f][step, pl.ds(off, 16)].astype(jnp.float32)
            target[pl.ds(here + off, 16)] = total.astype(target.dtype)
            return carry

        lax.fori_loop(0, rows // 16, body, 0)

    def to_other_core(step, carry):
        for f, flow in enumerate(flows):
            core_copy(f, shard_at(flow, step)).start()
        return carry

    lax.fori_loop(0, nodes, to_other_core, 0)

    def towards(step, carry):
        for f, flow in enumerate(flows):
            shard = shard_at(flow, step)
            core_copy(f, shard).wait_recv()
            if carry is None:
                add(f, shard, None, w_ref)
            else:
                ring_copy(f, step - 1, shard).wait_recv()
                add(f, shard, step - 1, w_ref)
            ring_copy(f, step, shard).start()
        return carry

    towards(0, None)
    count = s_ref.shape[0]

    def held(k):
        return s_ref if k == 0 else small_land.at[2 * k - 1]

    def small_copy(k):
        last = k == len(peers)
        return pltpu.make_async_remote_copy(
            src_ref=held(k), dst_ref=t_ref.at[pl.ds(count, count)] if last else small_land.at[2 * k],
            send_sem=small_send.at[k], recv_sem=small_recv.at[k],
            device_id=other_x if last else peers[k], device_id_type=MESH)

    def small_step(k):
        if 0 < k <= len(peers):
            small_copy(k - 1).wait_recv()
            small_land[2 * k - 1] = held(k - 1)[...] + small_land[2 * k - 2]
        if k <= len(peers):
            small_copy(k).start()
        if k == len(peers):
            t_ref[pl.ds(0, count)] = held(k)[...]

    small_step(0)
    for k in range(1, len(peers) + 1):
        if k < nodes - 1:
            towards(k, 0)
        small_step(k)
    lax.fori_loop(min(len(peers) + 1, nodes - 1), nodes - 1, towards, 0)
    for f, flow in enumerate(flows):
        shard = shard_at(flow, nodes - 1)
        core_copy(f, shard).wait_recv()
        ring_copy(f, nodes - 2, shard).wait_recv()
        add(f, shard, nodes - 2, o_ref)
        back_copy(f, 0, shard).start()
        over_copy(f, shard).start()

    def back(step, carry):
        for f, flow in enumerate(flows):
            shard = shard_at(flow, nodes - 1 + step)
            back_copy(f, step - 1, shard).wait_recv()
            back_copy(f, step, shard).start()
            over_copy(f, shard).start()
        return carry

    lax.fori_loop(1, nodes - 1, back, 0)
    for f, flow in enumerate(flows):
        shard = shard_at(flow, 2 * nodes - 2)
        back_copy(f, nodes - 2, shard).wait_recv()
        over_copy(f, shard).start()

    def settle(step, carry):
        for f, flow in enumerate(flows):
            core_copy(f, step).wait_send()
            over_copy(f, step).wait()
        return carry

    def settle_ring(step, carry):
        for f, flow in enumerate(flows):
            ring_copy(f, step, 0).wait_send()
            back_copy(f, step, 0).wait_send()
        return carry

    lax.fori_loop(0, nodes, settle, 0)
    lax.fori_loop(0, nodes - 1, settle_ring, 0)
    for k in range(len(peers) + 1):
        small_copy(k).wait_send()
    small_copy(len(peers)).wait_recv()


def sum_everywhere(big, small, ny, nz, cid=1):
    rows = big.shape[0]
    nodes = ny * nz
    sizes = ring_sizes(rows // 2, nodes)
    flows = [(w, i) for w in range(2) for i in range(len(sizes[w])) if sizes[w][i]]
    half = sum(map(sum, sizes)) * nodes
    assert rows == 2 * half, (rows, half, sizes)
    n = len(flows)
    return pl.pallas_call(
        functools.partial(ring_kernel, ny, nz, sizes),
        out_shape=(jax.ShapeDtypeStruct(big.shape, big.dtype),
                   jax.ShapeDtypeStruct((2 * small.shape[0], small.shape[1]), small.dtype)),
        in_specs=[pl.BlockSpec(memory_space=pltpu.VMEM)] * 2,
        out_specs=[pl.BlockSpec(memory_space=pltpu.VMEM)] * 2,
        scratch_shapes=[pltpu.VMEM((half, WIDE), big.dtype)]
        + [pltpu.VMEM((nodes - 1, sizes[w][i], WIDE), big.dtype) for w, i in flows]
        + [pltpu.VMEM((16,) + small.shape, small.dtype)]
        + [pltpu.SemaphoreType.DMA((n, nodes))] * 2
        + [pltpu.SemaphoreType.DMA((n, 2 * nodes - 2))] * 2
        + [pltpu.SemaphoreType.DMA((n, nodes))] * 2
        + [pltpu.SemaphoreType.DMA((8,))] * 2,
        compiler_params=pltpu.CompilerParams(collective_id=cid, has_side_effects=True, vmem_limit_bytes=56 << 20),
    )(big, small)


def shards(
    boundary, lengths, masked, residues, readout,
    first_gain, first_shift, in_weight, in_bias, second_gain, second_shift, conv_weight, conv_bias,
    third_gain, third_shift, out_weight, out_bias,
):
    ny, nz = lax.axis_size("seq") // 2, lax.axis_size("dp")
    width, hidden = in_weight.shape[1], in_weight.shape[2]
    count = (KERNEL + 2 * width // hidden) * hidden
    big_rows = 2 * ny * nz * sum(map(sum, ring_sizes(count // 2, ny * nz)))
    readout = jnp.pad(readout.T, ((0, 32 - VOCAB), (0, 0)))
    boundary_out, big, small = run_blocks(
        (
            boundary, lengths, masked, residues, readout,
            first_gain, first_shift, in_weight, in_bias, second_gain, second_shift, conv_weight, conv_bias,
            third_gain, third_shift, out_weight, out_bias,
        ),
        big_rows,
    )
    big, small = sum_everywhere(big, small, ny, nz)
    big = big.astype(jnp.float32)
    at = width + KERNEL * hidden
    grad_in_weight = big[None, :width]
    grad_conv_weight = big[width:at].reshape(conv_weight.shape)
    grad_out_weight = jnp.concatenate(
        [big[at + j : at + j + hidden] for j in range(0, width, hidden)], axis=1
    )[None]
    type_hits = small[6, :VOCAB] + small[14, :VOCAB]
    type_tally = small[7, :VOCAB] + small[15, :VOCAB]
    return (
        boundary_out,
        small[0:1],
        small[1:2],
        grad_in_weight,
        small[3:4, :hidden],
        small[3:4, hidden:],
        small[4:5, :hidden],
        grad_conv_weight,
        small[4:5, hidden:],
        small[5:6, :hidden],
        small[5:6, hidden:],
        grad_out_weight,
        small[2:3],
        type_hits / jnp.maximum(type_tally, 1.0),
        type_tally.astype(jnp.int32),
    )


def solution(mesh):
    in_specs = (
        P("section", "dp", "seq", None),
        P("dp", None),
        P("dp", "seq"),
        P("dp", "seq"),
        P(),
        P("section", None),
        P("section", None),
        P("section", None, None),
        P("section", None),
        P("section", None),
        P("section", None),
        P("section", None, None, None),
        P("section", None),
        P("section", None),
        P("section", None),
        P("section", None, None),
        P("section", None),
    )
    out_specs = (
        P("section", "dp", "seq", None),
        P("section", None),
        P("section", None),
        P("section", None, None),
        P("section", None),
        P("section", None),
        P("section", None),
        P("section", None, None, None),
        P("section", None),
        P("section", None),
        P("section", None),
        P("section", None, None),
        P("section", None),
        P(),
        P(),
    )
    return jax.shard_map(shards, mesh=mesh, in_specs=in_specs, out_specs=out_specs, check_vma=False)
```

time: 575 us -> 237 us (0.41)
  starting transfers between devices: 120 us -> 0 us
  matrix products: 117 us -> 0 us
  Pallas kernels: 92.9 us -> 209 us
  waiting for transfers between devices: 107 us -> 0 us
  other arithmetic: 88.7 us -> 12.8 us
  local copies, waits for them, and re-layouts: 39.8 us -> 13.9 us
    ppermute x48 -> x0, starting transfers between devices: 120 us -> none  [from_behind(): return lax.ppermute(value, axis, pairs)]
    pallas_call x0 -> x1, Pallas kernels: none -> 118 us  [run_blocks(): pl.pallas_call(functools.partial(blocks_kernel, edge), out_shape=(jax.Sha...]
    dot_general x50 -> x0, matrix products: 117 us -> none  [the longest x5 32.1 us: backward_block(): lax.dot_general(stacked, grad_second_low, contract, preferred_element_typ...]
    ppermute x48 -> x0, waiting for transfers between devices: 107 us -> none  [from_behind(): return lax.ppermute(value, axis, pairs)]
    reduce_sum x83 -> x0, other arithmetic: 45.3 us -> none  [the longest x12 20.5 us: norm_act(): average = jnp.mean(values, axis=-1, keepdims=True)]
    unnamed x194 -> x7, local copies, waits for them, and re-layouts: 21.4 us -> 1.5 us
    convert_element_type x25 -> x1, other arithmetic: 19.3 us -> 1.27 us  [shards(): type_tally.astype(jnp.int32)]
    unnamed x51 -> x1, other arithmetic: 9.22 us -> 0.01 us
  transfers between devices with their start and end apart: 48 -> 0, of which waited for: 16 -> 0; matrix products, arithmetic and copies ran while one was open for 13% -> 0% of each run, Pallas kernels for 0% -> 0%
where the time goes in v2:
time: 237 us
  Pallas kernels  209 us (88%)
  local copies, waits for them, and re-layouts  13.9 us (6%)
  other arithmetic  12.8 us (5%)
    pallas_call x1, Pallas kernels, run_blocks(): pl.pallas_call(functools.partial(blocks_kernel, edge), out_shape=(jax.Sha...  118 us
    pallas_call x1, Pallas kernels, sum_everywhere(): pl.pallas_call(functools.partial(ring_kernel, ny, nz, sizes), out_shape=(...  91.4 us
    convert_element_type x1, other arithmetic, shards(): big = big.astype(jnp.float32)  9.56 us

profile of v2, /device:TPU:0, one launch (start us, length us, event | category | flops | bytes accessed | tf_op | source)
XLA Modules:
  0.0 236.5 jit_solution(7908374162026418095)
XLA Ops:
  0.6 1.5 pad.4.readout
  2.2 117.7 %shard_map.280 = (bf16[1,4,256,1280]{3,2,1,0:T(8,128)(2,1)}, bf16[5888,640]{1,0:T(8,128)(2,1)}, f32[8,1280]{1,0:T(8,128)}) custom-call(bf16[1,4,256,1280]{3,2,1,0:T(8,128)(2,1)} %boundary.1, s32[4,4]{1,0:T(4,128)} %lengths.1, s32[4,256]{1,0:T(4,128)} %masked.1, s32[4,256]{1,0:T(4,128)} %residues.1, bf16[32,1280]{1,0:T(8,128)(2,1)} %pad.4.readout, ...), custom_call_target="tpu_custom_call" | custom-call | tf_op jit(solution)/shard_map/pallas_call | solution.py:458
  119.9 91.4 %shard_map.281 = (bf16[5888,640]{1,0:T(8,128)(2,1)}, f32[16,1280]{1,0:T(8,128)}) custom-call(bf16[5888,640]{1,0:T(8,128)(2,1)} %get-tuple-element.21.w_ref, f32[8,1280]{1,0:T(8,128)} %get-tuple-element.22.s_ref), custom_call_target="tpu_custom_call" | custom-call | tf_op jit(solution)/shard_map/pallas_call | solution.py:708
  211.3 1.5 fusion.2
  212.8 0.0 slice-start
  212.8 0.0 slice-start.1
  212.8 9.6 %convert_element_type.11 = f32[5888,640]{1,0:T(8,128)} convert(bf16[5888,640]{1,0:T(8,128)(2,1)} %get-tuple-element.24) | non-fusion elementwise | flops 3768320 | bytes 22609920 | tf_op jit(solution)/shard_map/convert_element_type | solution.py:744
  222.4 3.8 %slice_bitcast_fusion = f32[1,1280,640]{2,1,0:T(8,128)} fusion(f32[5888,640]{1,0:T(8,128)} %convert_element_type.11), kind=kLoop, calls=%fused_computation | loop fusion | bytes 6553600 | tf_op jit(solution)/shard_map/broadcast_in_dim | solution.py:746
  226.2 1.5 fusion.3
  227.7 0.0 slice-done
  227.7 0.0 slice-done.1
  227.7 3.9 %slice.69 = f32[3200,640]{1,0:T(8,128)} slice(bf16[5888,640]{1,0:T(8,128)(2,1)S(1)} %bitcast.11), slice={[1280:4480], [0:640]} | slice | bytes 16384000 | tf_op jit(solution)/shard_map/slice | solution.py:747
  231.6 0.2 fusion.1
  231.8 0.0 copy-start
  231.8 2.0 maximum_bitcast_fusion
  233.7 1.3 convert_bitcast_fusion
  235.0 0.0 copy-done
  235.0 1.5 copy.33
  (1 shorter events, 0.0 us)
Async XLA Ops:
  212.8 14.9 %slice-start = ((s8[7536640]{0:T(1024)(128)(4,1)}), s8[4194304]{0:T(1024)(128)(4,1)S(1)}, s32[]{:S(2)}) async-start(s8[7536640]{0:T(1024)(128)(4,1)} %bitcast.10), calls=%async_computation | async-start | bytes 8388608
  212.8 14.9 %slice-start.1 = ((s8[7536640]{0:T(1024)(128)(4,1)}), s8[3342336]{0:T(1024)(128)(4,1)S(1)}, s32[]{:S(2)}) async-start(s8[7536640]{0:T(1024)(128)(4,1)} %bitcast.10), calls=%async_computation.1 | async-start | bytes 6684672
  231.8 3.2 %copy-start = (bf16[1,4,256,1280]{3,2,1,0:T(8,128)(2,1)S(1)}, bf16[1,4,256,1280]{3,2,1,0:T(8,128)(2,1)}, u32[]{:S(2)}) copy-start(bf16[1,4,256,1280]{3,2,1,0:T(8,128)(2,1)} %get-tuple-element.53) | copy-start | bytes 7864324
